TPU v7x, 32 devices: a whole 2x2x4 slice. The times are simulated.
32 devices in a mesh: ep: 16 (over z, x, core), dp: 2 (over y).
Axes of the slice: x: 2, y: 2, z: 4, core: 2. Of those that a mesh axis runs over, the one named last changes fastest.
Arguments:
- tokens: bfloat16 [4096, 2048], P(('ep', 'dp')), may hold values from -6 to 6
- routes: int32 [4096, 8], P(('ep', 'dp')), may hold values from 0 to 15, as said below
- gates: bfloat16 [4096, 8], P(('ep', 'dp')), may hold values from 0.19921875 to 1
- w_gate: bfloat16 [16, 2048, 768], P('ep'), may hold values from -0.125 to 0.125
- w_up: bfloat16 [16, 2048, 768], P('ep'), may hold values from -0.125 to 0.125
- w_down: bfloat16 [16, 768, 2048], P('ep'), may hold values from -0.21875 to 0.21875
- score_head: float32 [2048], replicated, may hold values from -0.125 to 0.125
- doc_ids: int32 [32], P(('ep', 'dp')), may hold values from 0 to 7, never falling along the last dimension, each value on 1 to 8 neighbouring positions
Outputs:
- mixed: bfloat16 [4096, 2048], P(('ep', 'dp'))
- doc_scores: float32 [3, 8], replicated
Inputs may be any that keep to these rules, and one draw needn't show every extreme that they name: `routes`: each row names 8 different experts; among the rows of one device no expert is named more than 96 times. `doc_ids`: never falling along the passages; every document has 1 to 8 passages.
All inputs are finite; a program needn't handle non-finite values.
Results may differ from a plain program's by a relative error of at most 0.0058.
Values may be sent and summed in bfloat16 or wider, within the bound.
No kernel may reach another device: no remote copies, remote signals or barrier semaphores. Data moves between devices by JAX's collectives and lax.ppermute only.
A program may use at most 64 MiB of HBM per device.

v0:
```python
import functools
import math

import jax
import jax.numpy as jnp
from jax import lax
from jax.experimental import pallas as pl
from jax.experimental.pallas import tpu as pltpu
from jax.sharding import PartitionSpec as P

TOP = 8
PASSAGE = 128


def expert_rows(rows, gate_rows, wg_single, wu_single, wd_single):
    gate_part = jnp.dot(rows, wg_single, preferred_element_type=jnp.float32)
    up_part = jnp.dot(rows, wu_single, preferred_element_type=jnp.float32)
    hidden = (jax.nn.silu(gate_part) * up_part).astype(jnp.bfloat16)
    result = jnp.dot(hidden, wd_single, preferred_element_type=jnp.float32)
    return (gate_rows.astype(jnp.float32)[:, None] * result).astype(jnp.bfloat16)


def run_expert(slot_rows, slot_gates, wg_single, wu_single, wd_single):
    width = slot_rows.shape[-1]
    rows = slot_rows.reshape(-1, width)
    gate_rows = slot_gates.reshape(-1)
    result = expert_rows(rows, gate_rows, wg_single, wu_single, wd_single)
    return result.reshape(slot_rows.shape)


def slot_shards(tokens, routes, gates, w_gate, w_up, w_down, score_head, doc_ids):
    tok_dev, width = tokens.shape
    experts = lax.axis_size("ep")
    capacity = min(tok_dev, 3 * tok_dev * TOP // (2 * experts))
    flat_routes = routes.reshape(-1)
    onehot = (flat_routes[:, None] == jnp.arange(experts, dtype=jnp.int32)[None, :]).astype(
        jnp.int32
    )
    ranked = jnp.cumsum(onehot, axis=0)
    slot = jnp.sum(ranked * onehot, axis=1) - 1
    destination = flat_routes * capacity + slot
    repeated = jnp.repeat(tokens, TOP, axis=0)
    send_rows = jnp.zeros((experts * capacity, width), jnp.bfloat16).at[destination].set(repeated)
    send_gates = (
        jnp.zeros((experts * capacity,), jnp.bfloat16).at[destination].set(gates.reshape(-1))
    )
    recv_rows, recv_gates = (
        lax.all_to_all(
            send_rows.reshape(experts, capacity, width),
            "ep",
            split_axis=0,
            concat_axis=0,
            tiled=True,
        ),
        lax.all_to_all(
            send_gates.reshape(experts, capacity), "ep", split_axis=0, concat_axis=0, tiled=True
        ),
    )
    wg_single = w_gate[0]
    wu_single = w_up[0]
    wd_single = w_down[0]
    results = run_expert(recv_rows, recv_gates, wg_single, wu_single, wd_single)
    returned = lax.all_to_all(results, "ep", split_axis=0, concat_axis=0, tiled=True)
    returned_flat = returned.reshape(experts * capacity, width)
    gathered = returned_flat[destination].astype(jnp.float32).reshape(tok_dev, TOP, width)
    mixed = jnp.sum(gathered, axis=1).astype(jnp.bfloat16)
    token_score = jnp.dot(mixed.astype(jnp.float32), score_head, precision=lax.Precision.HIGHEST)
    passage_score = token_score.reshape(-1, PASSAGE).sum(axis=1) / math.sqrt(PASSAGE)
    doc_count = lax.axis_size("ep") * lax.axis_size("dp") * tok_dev // PASSAGE // 4
    doc_range = jnp.arange(doc_count, dtype=jnp.int32)[None, :]
    all_scores, all_docs = (
        lax.all_gather(passage_score, ("ep", "dp"), axis=0, tiled=True),
        lax.all_gather(doc_ids.astype(jnp.float32), ("ep", "dp"), axis=0, tiled=True),
    )
    member = all_docs[:, None] == doc_range.astype(jnp.float32)
    column = all_scores[:, None]
    passage_index = jnp.arange(all_scores.shape[0], dtype=jnp.int32)[:, None]
    max_score = jnp.where(member, column, -1e30).max(axis=0)
    sum_score = jnp.where(member, column, 0.0).sum(axis=0)
    first_index = jnp.where(member, passage_index, all_scores.shape[0]).min(axis=0)
    first_score = jnp.where(member & (passage_index == first_index[None, :]), column, 0.0).sum(
        axis=0
    )
    return (mixed, jnp.stack([max_score, first_score, sum_score]))


def pool(all_scores, all_docs, doc_count):
    doc_range = jnp.arange(doc_count, dtype=jnp.int32)[None, :]
    member = all_docs[:, None] == doc_range.astype(jnp.float32)
    column = all_scores[:, None]
    passage_index = jnp.arange(all_scores.shape[0], dtype=jnp.int32)[:, None]
    max_score = jnp.where(member, column, -1e30).max(axis=0)
    sum_score = jnp.where(member, column, 0.0).sum(axis=0)
    first_index = jnp.where(member, passage_index, all_scores.shape[0]).min(axis=0)
    first_score = jnp.where(member & (passage_index == first_index[None, :]), column, 0.0).sum(
        axis=0
    )
    return jnp.stack([max_score, first_score, sum_score])


LANES = 128


def tile_of(extent, most):
    return most if extent % most == 0 else extent


def expert_kernel(
    slot, xa, xb, wg0, wu0, wd0, wg1, wu1, wd1, gate, head, after, held,
    outa, outb, score, passed,
    rows, hidden, scale, x_sem,
):
    tok, width = xa.shape
    local = tok // PASSAGE
    out_tile = tile_of(width, 1024)
    blocks = [pl.ds(n * tok, tok) for n in range(2)]
    x_copies = [
        pltpu.make_async_copy(ref, rows.at[blocks[n], :], x_sem.at[n])
        for n, ref in enumerate((xa, xb))
    ]
    for copy in x_copies:
        copy.start()

    diagonal = lax.broadcasted_iota(jnp.int32, (tok, tok), 0) == lax.broadcasted_iota(
        jnp.int32, (tok, tok), 1
    )
    for n in range(2):
        for e in range(2):
            row = gate[pl.ds(2 * slot + n, 1), pl.ds(e * tok, tok)]
            scale[e, blocks[n], :] = jnp.sum(
                jnp.where(diagonal, row, 0.0), axis=1, keepdims=True
            )

    for copy in x_copies:
        copy.wait()
    for e, (wg, wu) in enumerate(((wg0, wu0), (wg1, wu1))):
        gate_part = jnp.dot(rows[...], wg[...], preferred_element_type=jnp.float32)
        up_part = jnp.dot(rows[...], wu[...], preferred_element_type=jnp.float32)
        value = gate_part / (1.0 + jnp.exp(-gate_part)) * up_part
        hidden[e] = value.astype(jnp.bfloat16)

    totals = [jnp.zeros((1, LANES), jnp.float32) for _ in range(2 * local)]
    for j in range(width // out_tile):
        columns = pl.ds(j * out_tile, out_tile)
        weighted = sum(
            scale[e] * jnp.dot(hidden[e], wd[:, columns], preferred_element_type=jnp.float32)
            for e, wd in enumerate((wd0, wd1))
        )
        rounded = weighted.astype(jnp.bfloat16)
        outa[:, columns] = rounded[:tok]
        outb[:, columns] = rounded[tok:]
        scored = weighted * head[:, columns]
        lanes = sum(
            scored[:, k * LANES : (k + 1) * LANES] for k in range(out_tile // LANES)
        )
        for p in range(2 * local):
            totals[p] += jnp.sum(lanes[p * PASSAGE : (p + 1) * PASSAGE], axis=0, keepdims=True)
    for p in range(2 * local):
        score[pl.ds(p, 1), :] = totals[p]


def load_kernel(count, *refs):
    refs = refs[-2 * count - 1 :]
    copies = [
        pltpu.make_async_copy(src, dst, refs[-1].at[n])
        for n, (src, dst) in enumerate(zip(refs[:count], refs[count:-1]))
    ]
    for copy in copies:
        copy.start()
    for copy in copies:
        copy.wait()


def load(arrays, *firsts):
    arrays = [pltpu.with_memory_space_constraint(a, pltpu.HBM) for a in arrays]
    return pl.pallas_call(
        functools.partial(load_kernel, len(arrays)),
        in_specs=[pl.BlockSpec(memory_space=pl.ANY)] * (len(firsts) + len(arrays)),
        out_specs=[pl.BlockSpec(memory_space=pltpu.VMEM)] * len(arrays),
        out_shape=[pltpu.VMEM(a.shape, a.dtype) for a in arrays],
        scratch_shapes=[pltpu.SemaphoreType.DMA((len(arrays),))],
        compiler_params=pltpu.CompilerParams(vmem_limit_bytes=2**20),
        name="load",
    )(*firsts, *arrays)


def tie_kernel(*refs):
    pass


def tie(value, *firsts):
    anywhere = pl.BlockSpec(memory_space=pl.ANY)
    return pl.pallas_call(
        tie_kernel,
        in_specs=[anywhere] * (1 + len(firsts)),
        out_specs=anywhere,
        out_shape=jax.ShapeDtypeStruct(value.shape, value.dtype),
        input_output_aliases={len(firsts): 0},
        compiler_params=pltpu.CompilerParams(vmem_limit_bytes=2**20),
        name="tie",
    )(*firsts, value)


def expert_call(slot, blocks, weights, gate, head, after, held):
    tok, width = blocks[0].shape
    ff = weights[0].shape[1]
    local = tok // PASSAGE
    anywhere = pl.BlockSpec(memory_space=pl.ANY)
    vmem = pl.BlockSpec(memory_space=pltpu.VMEM)
    bf16 = jnp.bfloat16
    return pl.pallas_call(
        functools.partial(expert_kernel, slot),
        in_specs=[anywhere] * 2 + [vmem] * 8 + [anywhere, anywhere],
        out_specs=[vmem, vmem, vmem, anywhere],
        out_shape=[
            pltpu.VMEM((tok, width), bf16),
            pltpu.VMEM((tok, width), bf16),
            jax.ShapeDtypeStruct((2 * local, LANES), jnp.float32),
            jax.ShapeDtypeStruct(held.shape, held.dtype),
        ],
        input_output_aliases={11: 3},
        scratch_shapes=[
            pltpu.VMEM((2 * tok, width), bf16),
            pltpu.VMEM((2, 2 * tok, ff), bf16),
            pltpu.VMEM((2, 2 * tok, 1), jnp.float32),
            pltpu.SemaphoreType.DMA((2,)),
        ],
        compiler_params=pltpu.CompilerParams(vmem_limit_bytes=16 * 2**20),
        cost_estimate=pl.CostEstimate(flops=1, bytes_accessed=1, transcendentals=0),
        name="expert",
    )(*blocks, *weights, gate, head, after, held)


def dense_shards(tokens, routes, gates, w_gate, w_up, w_down, score_head, doc_ids):
    tok_dev, width = tokens.shape
    experts = lax.axis_size("ep")
    groups = lax.axis_size("dp")
    local = tok_dev // PASSAGE
    ring = experts // 4
    me = lax.axis_index("ep")
    places = [*range(0, ring, 2), *reversed(range(1, ring, 2))]
    onward = lambda v: lax.ppermute(
        v,
        "ep",
        [
            (4 * places[n] + i, 4 * places[(n + 1) % ring] + i)
            for n in range(ring)
            for i in range(4)
        ],
    )
    across = lambda v: lax.ppermute(v, "ep", [(i, i ^ 2) for i in range(experts)])
    sibling = lambda v: lax.ppermute(v, "ep", [(i, i ^ 1) for i in range(experts)])

    own = (w_gate[0], w_up[0], w_down[0])

    cores = [[2 * n + core for n in range(experts // 2)] for core in range(2)]
    target = jnp.arange(experts, dtype=jnp.int32)
    wanted = (target // 2 * 2 + me % 2) ^ target % 2
    chosen = routes.T[:, None, :] == wanted[None, :, None]
    sent_gates = jnp.where(chosen, gates.T[:, None, :], jnp.bfloat16(0)).sum(axis=0)
    sent_gates = sent_gates.reshape(experts // 2, 2 * tok_dev)
    gate_rows = lax.all_to_all(
        sent_gates, "ep", split_axis=0, concat_axis=0, tiled=True, axis_index_groups=cores
    )
    row = jnp.arange(2 * ring, dtype=jnp.int32)
    z = me // 4
    at = jnp.where(z % 2 == 0, z // 2, ring - (z + 1) // 2)
    back = lax.rem(at - row // 2 + ring, ring)
    back = jnp.where(back < (ring + 1) // 2, 2 * back, 2 * (ring - back) - 1)
    order = back * 4 + (me % 4 ^ row % 2 * 2)
    position = order[:, None] == jnp.arange(experts, dtype=jnp.int32)[None, :]
    slot_gates = gate_rows.astype(jnp.float32)[order // 2]

    near = [tokens]
    coming = [onward(tokens)]
    far = [across(tokens)]

    def step(*meanwhile):
        near.append(tie(coming[-1], far[-1], *meanwhile))
        if len(near) < ring:
            coming.append(onward(near[-1]))
            far.append(across(near[-1]))
        else:
            far.append(onward(far[-1]))

    head = score_head[None, :]
    scores = [None] * ring
    mine = [None] * ring
    other = [None] * ring

    def work(s, after, held):
        mine[s], other[s], scores[s], passed = expert_call(
            s, (near[s], far[s]), weights, slot_gates, head, after, held
        )
        return passed

    step(slot_gates)
    weights = load(own, slot_gates)
    step(weights[0])
    weights = weights + load([sibling(w) for w in own], slot_gates)
    weights = [pltpu.with_memory_space_constraint(w, pltpu.VMEM) for w in weights]
    held = jnp.zeros((8, LANES), jnp.float32)
    turns = [1, 0, *range(2, ring)]
    for n, s in enumerate(turns):
        if n == ring - 1:
            other[0] = work(s, held, other[0])
        else:
            held = work(s, near[-1], held)
        if len(near) < ring:
            step(scores[s])
    carried = None
    sent = []
    for s in [*range(1, ring), 0]:
        crossing = tie(other[0], sent[-1]) if s == 0 else other[s]
        total = mine[s].astype(jnp.float32) + across(crossing).astype(jnp.float32)
        if carried is not None:
            total = total + carried.astype(jnp.float32)
        total = total.astype(jnp.bfloat16)
        if s > 0:
            carried = onward(total)
            sent.append(total)
    mixed = total

    slot_scores = jnp.stack(scores).sum(axis=2).reshape(2 * ring, local) / math.sqrt(PASSAGE)
    part_score = jnp.where(position[:, :, None], slot_scores[:, None, :], 0.0).sum(axis=0)
    told = jnp.concatenate([part_score.reshape(-1), doc_ids.astype(jnp.float32)])
    told = jnp.pad(told, (0, -told.shape[0] % LANES))[None, :]
    told = tie(told, sent[-2])
    heard = lax.all_to_all(
        jnp.broadcast_to(told, (experts * groups, told.shape[1])),
        ("ep", "dp"),
        split_axis=0,
        concat_axis=0,
        tiled=True,
    )
    count = experts * local
    all_scores = heard[:, :count].reshape(experts, groups, experts, local).sum(axis=0)
    all_scores = all_scores.transpose(1, 0, 2).reshape(-1)
    all_docs = heard[:, count : count + local].reshape(-1)
    return (mixed, pool(all_scores, all_docs, count * groups // 4))


def shards(tokens, *rest):
    tok_dev = tokens.shape[0]
    experts = lax.axis_size("ep")
    capacity = min(tok_dev, 3 * tok_dev * TOP // (2 * experts))
    dense = 2 * capacity >= tok_dev and experts % 4 == 0 and tok_dev % PASSAGE == 0
    return (dense_shards if dense else slot_shards)(tokens, *rest)


def solution(mesh):
    return jax.shard_map(
        shards,
        mesh=mesh,
        in_specs=(
            P(("ep", "dp"), None),
            P(("ep", "dp"), None),
            P(("ep", "dp"), None),
            P("ep", None, None),
            P("ep", None, None),
            P("ep", None, None),
            P(),
            P(("ep", "dp")),
        ),
        out_specs=(P(("ep", "dp"), None), P()),
        check_vma=False,
    )
```

profile of v0, /device:TPU:0, one launch (start us, length us, event | category | flops | bytes accessed | tf_op | source)
XLA Modules:
  0.0 100.2 jit_solution(10156955141333087107)
XLA Ops:
  1.7 2.6 %collective-permute-start = (bf16[128,2048]{1,0:T(8,128)(2,1)}, bf16[128,2048]{1,0:T(8,128)(2,1)S(1)}, u32[]{:S(2)}, u32[]{:S(2)}) collective-permute-start(bf16[128,2048]{1,0:T(8,128)(2,1)} %xa.1), channel_id=1, source_target_pairs={{0,4},{2,6},{4,0},{6,2},{8,12},{10,14},{12,8},{14,10},{16,20},{18,... | collective-permute-start | bytes 1572872 | tf_op jit(solution)/shard_map/ppermute | solution.py:251
  4.2 2.6 %collective-permute-start.4 = (bf16[128,2048]{1,0:T(8,128)(2,1)}, bf16[128,2048]{1,0:T(8,128)(2,1)S(1)}, u32[]{:S(2)}, u32[]{:S(2)}) collective-permute-start(bf16[128,2048]{1,0:T(8,128)(2,1)} %xa.1), channel_id=1, source_target_pairs={{0,16},{2,18},{4,20},{6,22},{16,24},{18,26},{20,28},{22,30},{24,8}... | collective-permute-start | bytes 1572872 | tf_op jit(solution)/shard_map/ppermute | solution.py:242
  9.4 3.3 %all-to-all-start = ((bf16[8,2,128]{2,1,0:T(2,128)(2,1)}), bf16[8,2,128]{2,1,0:T(2,128)(2,1)S(1)}, u32[]{:S(2)}, u32[]{:S(2)}) async-start(bf16[8,2,128]{2,1,0:T(2,128)(2,1)} %reshape.293), calls=%async_computation | async-start | bytes 8192 | tf_op jit(solution)/shard_map/all_to_all | solution.py:262
  12.8 7.6 %all-to-all-done = bf16[8,2,128]{2,1,0:T(2,128)(2,1)S(1)} async-done(((bf16[8,2,128]{2,1,0:T(2,128)(2,1)}), bf16[8,2,128]{2,1,0:T(2,128)(2,1)S(1)}, u32[]{:S(2)}, u32[]{:S(2)}) %all-to-all-start) | async-done | bytes 4128 | tf_op jit(solution)/shard_map/all_to_all | solution.py:262
  21.0 1.7 %collective-permute-start.6 = (bf16[128,2048]{1,0:T(8,128)(2,1)S(1)}, bf16[128,2048]{1,0:T(8,128)(2,1)S(1)}, u32[]{:S(2)}, u32[]{:S(2)}) collective-permute-start(bf16[128,2048]{1,0:T(8,128)(2,1)S(1)} %tie.5.xa), channel_id=1, source_target_pairs={{0,16},{2,18},{4,20},{6,22},{16,24},{18,26},{20,28},{22,30},{24,8}... | collective-permute-start | bytes 1572872 | tf_op jit(solution)/shard_map/ppermute | solution.py:242
  22.7 1.4 %collective-permute-start.5 = (bf16[128,2048]{1,0:T(8,128)(2,1)S(1)}, bf16[128,2048]{1,0:T(8,128)(2,1)S(1)}, u32[]{:S(2)}, u32[]{:S(2)}) collective-permute-start(bf16[128,2048]{1,0:T(8,128)(2,1)S(1)} %tie.5.xa), channel_id=1, source_target_pairs={{0,4},{2,6},{4,0},{6,2},{8,12},{10,14},{12,8},{14,10},{16,20},{18,... | collective-permute-start | bytes 1572872 | tf_op jit(solution)/shard_map/ppermute | solution.py:251
  24.1 3.8 %load.2 = (bf16[2048,768]{1,0:T(8,128)(2,1)S(1)}, bf16[2048,768]{1,0:T(8,128)(2,1)S(1)}, bf16[768,2048]{1,0:T(8,128)(2,1)S(1)}) custom-call(f32[8,256]{1,0:T(8,128)S(1)} %gather_fusion, bf16[2048,768]{1,0:T(8,128)(2,1)} %bitcast.39, bf16[2048,768]{1,0:T(8,128)(2,1)} %bitcast.41, bf16[768,2048]{1,0:T(8,128)(2,1)} %bitcast.43), custom_call_target="tpu_custom_call" | custom-call | tf_op jit(solution)/shard_map/load/pallas_call | solution.py:176
  27.9 6.1 %collective-permute-done.6.refs_2_ = bf16[128,2048]{1,0:T(8,128)(2,1)S(1)} collective-permute-done((bf16[128,2048]{1,0:T(8,128)(2,1)S(1)}, bf16[128,2048]{1,0:T(8,128)(2,1)S(1)}, u32[]{:S(2)}, u32[]{:S(2)}) %collective-permute-start.6) | collective-permute-done | bytes 524320 | tf_op jit(solution)/shard_map/ppermute | solution.py:242
  34.0 1.5 %collective-permute-done.5.refs_0_.xb = bf16[128,2048]{1,0:T(8,128)(2,1)S(1)} collective-permute-done((bf16[128,2048]{1,0:T(8,128)(2,1)S(1)}, bf16[128,2048]{1,0:T(8,128)(2,1)S(1)}, u32[]{:S(2)}, u32[]{:S(2)}) %collective-permute-start.5) | collective-permute-done | bytes 524320 | tf_op jit(solution)/shard_map/ppermute | solution.py:251
  36.7 1.4 %collective-permute-start.7 = (bf16[128,2048]{1,0:T(8,128)(2,1)S(1)}, bf16[128,2048]{1,0:T(8,128)(2,1)S(1)}, u32[]{:S(2)}, u32[]{:S(2)}) collective-permute-start(bf16[128,2048]{1,0:T(8,128)(2,1)S(1)} %tie.6.after.xa), channel_id=1, source_target_pairs={{0,4},{2,6},{4,0},{6,2},{8,12},{10,14},{12,8},{14,10},{16,20},{18,... | collective-permute-start | bytes 1572872 | tf_op jit(solution)/shard_map/ppermute | solution.py:251
  38.1 3.8 %load.3 = (bf16[2048,768]{1,0:T(8,128)(2,1)S(1)}, bf16[2048,768]{1,0:T(8,128)(2,1)S(1)}, bf16[768,2048]{1,0:T(8,128)(2,1)S(1)}) custom-call(f32[8,256]{1,0:T(8,128)S(1)} %gather_fusion, bf16[2048,768]{1,0:T(8,128)(2,1)} %collective-permute-done.1.refs_1_, bf16[2048,768]{1,0:T(8,128)(2,1)} %collective-permute-done.2.refs_2_, ...), custom_call_target="tpu_custom_call" | custom-call | tf_op jit(solution)/shard_map/load/pallas_call | solution.py:176
  42.0 5.7 %expert.4 = (bf16[128,2048]{1,0:T(8,128)(2,1)S(1)}, bf16[128,2048]{1,0:T(8,128)(2,1)S(1)}, f32[2,128]{1,0:T(2,128)S(1)}, f32[8,128]{1,0:T(8,128)S(1)}) custom-call(bf16[128,2048]{1,0:T(8,128)(2,1)S(1)} %tie.5.xa, bf16[128,2048]{1,0:T(8,128)(2,1)S(1)} %collective-permute-done.5.refs_0_.xb, ...), custom_call_target="tpu_custom_call", output_to_operand_aliasing={{3}: (11, {})} | custom-call | flops 1 | bytes 1 | tf_op jit(solution)/shard_map/expert/pallas_call | solution.py:211
  50.0 5.7 %expert.5 = (bf16[128,2048]{1,0:T(8,128)(2,1)S(1)}, bf16[128,2048]{1,0:T(8,128)(2,1)S(1)}, f32[2,128]{1,0:T(2,128)S(1)}, f32[8,128]{1,0:T(8,128)S(1)}) custom-call(bf16[128,2048]{1,0:T(8,128)(2,1)S(1)} %copy-done, bf16[128,2048]{1,0:T(8,128)(2,1)S(1)} %collective-permute-done.refs_0_.xb, ...), custom_call_target="tpu_custom_call", output_to_operand_aliasing={{3}: (11, {})} | custom-call | flops 1 | bytes 1 | tf_op jit(solution)/shard_map/expert/pallas_call | solution.py:211
  55.7 5.7 %expert.6 = (bf16[128,2048]{1,0:T(8,128)(2,1)S(1)}, bf16[128,2048]{1,0:T(8,128)(2,1)S(1)}, f32[2,128]{1,0:T(2,128)S(1)}, f32[8,128]{1,0:T(8,128)S(1)}) custom-call(bf16[128,2048]{1,0:T(8,128)(2,1)S(1)} %tie.6.after.xa, bf16[128,2048]{1,0:T(8,128)(2,1)S(1)} %collective-permute-done.7.refs_0_.xb, ...), custom_call_target="tpu_custom_call", output_to_operand_aliasing={{3}: (11, {})} | custom-call | flops 1 | bytes 1 | tf_op jit(solution)/shard_map/expert/pallas_call | solution.py:211
  61.3 1.2 %collective-permute-start.11 = (bf16[128,2048]{1,0:T(8,128)(2,1)S(1)}, bf16[128,2048]{1,0:T(8,128)(2,1)S(1)}, u32[]{:S(2)}, u32[]{:S(2)}) collective-permute-start(bf16[128,2048]{1,0:T(8,128)(2,1)S(1)} %get-tuple-element.39), channel_id=1, source_target_pairs={{0,4},{2,6},{4,0},{6,2},{8,12},{10,14},{12,8},{14,10},{16,20},{18,... | collective-permute-start | bytes 1572872 | tf_op jit(solution)/shard_map/ppermute | solution.py:251
  62.6 1.7 %collective-permute-start.13 = (bf16[128,2048]{1,0:T(8,128)(2,1)S(1)}, bf16[128,2048]{1,0:T(8,128)(2,1)S(1)}, u32[]{:S(2)}, u32[]{:S(2)}) collective-permute-start(bf16[128,2048]{1,0:T(8,128)(2,1)S(1)} %add_convert_fusion.3), channel_id=1, source_target_pairs={{0,16},{2,18},{4,20},{6,22},{16,24},{18,26},{20,28},{22,30},{24,8}... | collective-permute-start | bytes 1572872 | tf_op jit(solution)/shard_map/ppermute | solution.py:242
  65.0 5.7 %expert.7 = (bf16[128,2048]{1,0:T(8,128)(2,1)S(1)}, bf16[128,2048]{1,0:T(8,128)(2,1)S(1)}, f32[2,128]{1,0:T(2,128)S(1)}, bf16[128,2048]{1,0:T(8,128)(2,1)S(1)}) custom-call(bf16[128,2048]{1,0:T(8,128)(2,1)S(1)} %tie.7.after.xa, bf16[128,2048]{1,0:T(8,128)(2,1)S(1)} %collective-permute-done.9.xb, ...), custom_call_target="tpu_custom_call", output_to_operand_aliasing={{3}: (11, {})} | custom-call | flops 1 | bytes 1 | tf_op jit(solution)/shard_map/expert/pallas_call | solution.py:211
  71.7 2.1 %collective-permute-done.11 = bf16[128,2048]{1,0:T(8,128)(2,1)S(1)} collective-permute-done((bf16[128,2048]{1,0:T(8,128)(2,1)S(1)}, bf16[128,2048]{1,0:T(8,128)(2,1)S(1)}, u32[]{:S(2)}, u32[]{:S(2)}) %collective-permute-start.11) | collective-permute-done | bytes 524320 | tf_op jit(solution)/shard_map/ppermute | solution.py:251
  74.4 2.1 %collective-permute-start.14 = (bf16[128,2048]{1,0:T(8,128)(2,1)S(1)}, bf16[128,2048]{1,0:T(8,128)(2,1)}, u32[]{:S(2)}, u32[]{:S(2)}) collective-permute-start(bf16[128,2048]{1,0:T(8,128)(2,1)S(1)} %add_convert_fusion.2.refs_0_), channel_id=1, source_target_pairs={{0,16},{2,18},{4,20},{6,22},{16,24},{18,26},{20,28},{22,30},{24,8}... | collective-permute-start | bytes 1572872 | tf_op jit(solution)/shard_map/ppermute | solution.py:242
  77.4 4.0 %all-to-all-start.1 = ((f32[32,1,128]{2,1,0:T(1,128)}), f32[32,1,128]{2,1,0:T(1,128)S(1)}, u32[]{:S(2)}, u32[]{:S(2)}) async-start(f32[32,1,128]{2,1,0:T(1,128)} %broadcast_in_dim.90), calls=%async_computation.1 | async-start | bytes 32768 | tf_op jit(solution)/shard_map/all_to_all | solution.py:329
  82.6 1.3 %collective-permute-done.14 = bf16[128,2048]{1,0:T(8,128)(2,1)} collective-permute-done((bf16[128,2048]{1,0:T(8,128)(2,1)S(1)}, bf16[128,2048]{1,0:T(8,128)(2,1)}, u32[]{:S(2)}, u32[]{:S(2)}) %collective-permute-start.14) | collective-permute-done | bytes 524320 | tf_op jit(solution)/shard_map/ppermute | solution.py:242
  83.8 1.3 %add_convert_fusion.1.refs_0_ = bf16[128,2048]{1,0:T(8,128)(2,1)S(1)} fusion(bf16[128,2048]{1,0:T(8,128)(2,1)} %collective-permute-done.14, bf16[128,2048]{1,0:T(8,128)(2,1)S(1)} %collective-permute-done.10, bf16[128,2048]{1,0:T(8,128)(2,1)S(1)} %get-tuple-element.36), kind=kLoop, calls=%fused_computation.2 | loop fusion | flops 1572864 | bytes 2097152 | tf_op jit(solution)/shard_map/convert_element_type | solution.py:318
  85.1 3.1 %collective-permute-start.16 = (bf16[128,2048]{1,0:T(8,128)(2,1)S(1)}, bf16[128,2048]{1,0:T(8,128)(2,1)S(1)}, u32[]{:S(2)}, u32[]{:S(2)}) collective-permute-start(bf16[128,2048]{1,0:T(8,128)(2,1)S(1)} %add_convert_fusion.1.refs_0_), channel_id=1, source_target_pairs={{0,16},{2,18},{4,20},{6,22},{16,24},{18,26},{20,28},{22,30},{24,8}... | collective-permute-start | bytes 1572872 | tf_op jit(solution)/shard_map/ppermute | solution.py:242
  90.4 8.8 %collective-permute-done.15 = bf16[128,2048]{1,0:T(8,128)(2,1)S(1)} collective-permute-done((bf16[128,2048]{1,0:T(8,128)(2,1)S(1)}, bf16[128,2048]{1,0:T(8,128)(2,1)S(1)}, u32[]{:S(2)}, u32[]{:S(2)}) %collective-permute-start.15) | collective-permute-done | bytes 524320 | tf_op jit(solution)/shard_map/ppermute | solution.py:251
  (60 shorter events, 14.9 us)
Async XLA Ops:
  0.6 37.5 %collective-permute-start.1 = (bf16[2048,768]{1,0:T(8,128)(2,1)}, bf16[2048,768]{1,0:T(8,128)(2,1)}, u32[]{:S(2)}, u32[]{:S(2)}) collective-permute-start(bf16[2048,768]{1,0:T(8,128)(2,1)} %bitcast.38), channel_id=1, source_target_pairs={{0,2},{2,0},{4,6},{6,4},{8,10},{10,8},{12,14},{14,12},{16,18},{18,... | collective-permute-start | bytes 9437192 | tf_op jit(solution)/shard_map/ppermute | solution.py:252
  1.1 37.0 %collective-permute-start.2 = (bf16[2048,768]{1,0:T(8,128)(2,1)}, bf16[2048,768]{1,0:T(8,128)(2,1)}, u32[]{:S(2)}, u32[]{:S(2)}) collective-permute-start(bf16[2048,768]{1,0:T(8,128)(2,1)} %bitcast.40), channel_id=1, source_target_pairs={{0,2},{2,0},{4,6},{6,4},{8,10},{10,8},{12,14},{14,12},{16,18},{18,... | collective-permute-start | bytes 9437192 | tf_op jit(solution)/shard_map/ppermute | solution.py:252
  1.2 36.9 %collective-permute-start.3 = (bf16[768,2048]{1,0:T(8,128)(2,1)}, bf16[768,2048]{1,0:T(8,128)(2,1)}, u32[]{:S(2)}, u32[]{:S(2)}) collective-permute-start(bf16[768,2048]{1,0:T(8,128)(2,1)} %bitcast.42), channel_id=1, source_target_pairs={{0,2},{2,0},{4,6},{6,4},{8,10},{10,8},{12,14},{14,12},{16,18},{18,... | collective-permute-start | bytes 9437192 | tf_op jit(solution)/shard_map/ppermute | solution.py:252
  1.7 19.3 %collective-permute-start = (bf16[128,2048]{1,0:T(8,128)(2,1)}, bf16[128,2048]{1,0:T(8,128)(2,1)S(1)}, u32[]{:S(2)}, u32[]{:S(2)}) collective-permute-start(bf16[128,2048]{1,0:T(8,128)(2,1)} %xa.1), channel_id=1, source_target_pairs={{0,4},{2,6},{4,0},{6,2},{8,12},{10,14},{12,8},{14,10},{16,20},{18,... | collective-permute-start | bytes 1572872 | tf_op jit(solution)/shard_map/ppermute | solution.py:251
  4.2 16.8 %collective-permute-start.4 = (bf16[128,2048]{1,0:T(8,128)(2,1)}, bf16[128,2048]{1,0:T(8,128)(2,1)S(1)}, u32[]{:S(2)}, u32[]{:S(2)}) collective-permute-start(bf16[128,2048]{1,0:T(8,128)(2,1)} %xa.1), channel_id=1, source_target_pairs={{0,16},{2,18},{4,20},{6,22},{16,24},{18,26},{20,28},{22,30},{24,8}... | collective-permute-start | bytes 1572872 | tf_op jit(solution)/shard_map/ppermute | solution.py:242
  9.4 11.0 %all-to-all-start = ((bf16[8,2,128]{2,1,0:T(2,128)(2,1)}), bf16[8,2,128]{2,1,0:T(2,128)(2,1)S(1)}, u32[]{:S(2)}, u32[]{:S(2)}) async-start(bf16[8,2,128]{2,1,0:T(2,128)(2,1)} %reshape.293), calls=%async_computation | async-start | bytes 8192 | tf_op jit(solution)/shard_map/all_to_all | solution.py:262
  21.0 12.9 %collective-permute-start.6 = (bf16[128,2048]{1,0:T(8,128)(2,1)S(1)}, bf16[128,2048]{1,0:T(8,128)(2,1)S(1)}, u32[]{:S(2)}, u32[]{:S(2)}) collective-permute-start(bf16[128,2048]{1,0:T(8,128)(2,1)S(1)} %tie.5.xa), channel_id=1, source_target_pairs={{0,16},{2,18},{4,20},{6,22},{16,24},{18,26},{20,28},{22,30},{24,8}... | collective-permute-start | bytes 1572872 | tf_op jit(solution)/shard_map/ppermute | solution.py:242
  22.7 12.8 %collective-permute-start.5 = (bf16[128,2048]{1,0:T(8,128)(2,1)S(1)}, bf16[128,2048]{1,0:T(8,128)(2,1)S(1)}, u32[]{:S(2)}, u32[]{:S(2)}) collective-permute-start(bf16[128,2048]{1,0:T(8,128)(2,1)S(1)} %tie.5.xa), channel_id=1, source_target_pairs={{0,4},{2,6},{4,0},{6,2},{8,12},{10,14},{12,8},{14,10},{16,20},{18,... | collective-permute-start | bytes 1572872 | tf_op jit(solution)/shard_map/ppermute | solution.py:251
  35.5 6.4 %copy-start.1 = (f32[2048]{0:T(1024)S(1)}, f32[2048]{0:T(1024)}, u32[]{:S(2)}) copy-start(f32[2048]{0:T(1024)} %param.14) | copy-start | bytes 24580
  35.5 14.5 %collective-permute-start.8 = (bf16[128,2048]{1,0:T(8,128)(2,1)S(1)}, bf16[128,2048]{1,0:T(8,128)(2,1)S(1)}, u32[]{:S(2)}, u32[]{:S(2)}) collective-permute-start(bf16[128,2048]{1,0:T(8,128)(2,1)S(1)} %tie.6.after.xa), channel_id=1, source_target_pairs={{0,16},{2,18},{4,20},{6,22},{16,24},{18,26},{20,28},{22,30},{24,8}... | collective-permute-start | bytes 1572872 | tf_op jit(solution)/shard_map/ppermute | solution.py:242
  36.7 12.7 %collective-permute-start.7 = (bf16[128,2048]{1,0:T(8,128)(2,1)S(1)}, bf16[128,2048]{1,0:T(8,128)(2,1)S(1)}, u32[]{:S(2)}, u32[]{:S(2)}) collective-permute-start(bf16[128,2048]{1,0:T(8,128)(2,1)S(1)} %tie.6.after.xa), channel_id=1, source_target_pairs={{0,4},{2,6},{4,0},{6,2},{8,12},{10,14},{12,8},{14,10},{16,20},{18,... | collective-permute-start | bytes 1572872 | tf_op jit(solution)/shard_map/ppermute | solution.py:251
  41.9 8.0 %copy-start = (bf16[128,2048]{1,0:T(8,128)(2,1)S(1)}, bf16[128,2048]{1,0:T(8,128)(2,1)}, u32[]{:S(2)}) copy-start(bf16[128,2048]{1,0:T(8,128)(2,1)} %xa.1) | copy-start | bytes 1572868
  47.6 14.9 %collective-permute-start.12 = (bf16[128,2048]{1,0:T(8,128)(2,1)S(1)}, bf16[128,2048]{1,0:T(8,128)(2,1)S(1)}, u32[]{:S(2)}, u32[]{:S(2)}) collective-permute-start(bf16[128,2048]{1,0:T(8,128)(2,1)S(1)} %get-tuple-element.41), channel_id=1, source_target_pairs={{0,4},{2,6},{4,0},{6,2},{8,12},{10,14},{12,8},{14,10},{16,20},{18,... | collective-permute-start | bytes 1572872 | tf_op jit(solution)/shard_map/ppermute | solution.py:251
  49.4 15.6 %collective-permute-start.9 = (bf16[128,2048]{1,0:T(8,128)(2,1)S(1)}, bf16[128,2048]{1,0:T(8,128)(2,1)S(1)}, u32[]{:S(2)}, u32[]{:S(2)}) collective-permute-start(bf16[128,2048]{1,0:T(8,128)(2,1)S(1)} %collective-permute-done.7.refs_0_.xb), channel_id=1, source_target_pairs={{0,16},{2,18},{4,20},{6,22},{16,24},{18,26},{20,28},{22,30},{24,8}... | collective-permute-start | bytes 1572872 | tf_op jit(solution)/shard_map/ppermute | solution.py:242
  61.3 12.4 %collective-permute-start.11 = (bf16[128,2048]{1,0:T(8,128)(2,1)S(1)}, bf16[128,2048]{1,0:T(8,128)(2,1)S(1)}, u32[]{:S(2)}, u32[]{:S(2)}) collective-permute-start(bf16[128,2048]{1,0:T(8,128)(2,1)S(1)} %get-tuple-element.39), channel_id=1, source_target_pairs={{0,4},{2,6},{4,0},{6,2},{8,12},{10,14},{12,8},{14,10},{16,20},{18,... | collective-permute-start | bytes 1572872 | tf_op jit(solution)/shard_map/ppermute | solution.py:251
  62.6 11.5 %collective-permute-start.13 = (bf16[128,2048]{1,0:T(8,128)(2,1)S(1)}, bf16[128,2048]{1,0:T(8,128)(2,1)S(1)}, u32[]{:S(2)}, u32[]{:S(2)}) collective-permute-start(bf16[128,2048]{1,0:T(8,128)(2,1)S(1)} %add_convert_fusion.3), channel_id=1, source_target_pairs={{0,16},{2,18},{4,20},{6,22},{16,24},{18,26},{20,28},{22,30},{24,8}... | collective-permute-start | bytes 1572872 | tf_op jit(solution)/shard_map/ppermute | solution.py:242
  70.7 11.9 %collective-permute-start.10 = (bf16[128,2048]{1,0:T(8,128)(2,1)S(1)}, bf16[128,2048]{1,0:T(8,128)(2,1)S(1)}, u32[]{:S(2)}, u32[]{:S(2)}) collective-permute-start(bf16[128,2048]{1,0:T(8,128)(2,1)S(1)} %get-tuple-element.37), channel_id=1, source_target_pairs={{0,4},{2,6},{4,0},{6,2},{8,12},{10,14},{12,8},{14,10},{16,20},{18,... | collective-permute-start | bytes 1572872 | tf_op jit(solution)/shard_map/ppermute | solution.py:251
  74.4 9.5 %collective-permute-start.14 = (bf16[128,2048]{1,0:T(8,128)(2,1)S(1)}, bf16[128,2048]{1,0:T(8,128)(2,1)}, u32[]{:S(2)}, u32[]{:S(2)}) collective-permute-start(bf16[128,2048]{1,0:T(8,128)(2,1)S(1)} %add_convert_fusion.2.refs_0_), channel_id=1, source_target_pairs={{0,16},{2,18},{4,20},{6,22},{16,24},{18,26},{20,28},{22,30},{24,8}... | collective-permute-start | bytes 1572872 | tf_op jit(solution)/shard_map/ppermute | solution.py:242
  77.4 11.6 %all-to-all-start.1 = ((f32[32,1,128]{2,1,0:T(1,128)}), f32[32,1,128]{2,1,0:T(1,128)S(1)}, u32[]{:S(2)}, u32[]{:S(2)}) async-start(f32[32,1,128]{2,1,0:T(1,128)} %broadcast_in_dim.90), calls=%async_computation.1 | async-start | bytes 32768 | tf_op jit(solution)/shard_map/all_to_all | solution.py:329
  85.1 14.1 %collective-permute-start.16 = (bf16[128,2048]{1,0:T(8,128)(2,1)S(1)}, bf16[128,2048]{1,0:T(8,128)(2,1)S(1)}, u32[]{:S(2)}, u32[]{:S(2)}) collective-permute-start(bf16[128,2048]{1,0:T(8,128)(2,1)S(1)} %add_convert_fusion.1.refs_0_), channel_id=1, source_target_pairs={{0,16},{2,18},{4,20},{6,22},{16,24},{18,26},{20,28},{22,30},{24,8}... | collective-permute-start | bytes 1572872 | tf_op jit(solution)/shard_map/ppermute | solution.py:242
  88.2 11.0 %collective-permute-start.15 = (bf16[128,2048]{1,0:T(8,128)(2,1)S(1)}, bf16[128,2048]{1,0:T(8,128)(2,1)S(1)}, u32[]{:S(2)}, u32[]{:S(2)}) collective-permute-start(bf16[128,2048]{1,0:T(8,128)(2,1)S(1)} %tie.8), channel_id=1, source_target_pairs={{0,4},{2,6},{4,0},{6,2},{8,12},{10,14},{12,8},{14,10},{16,20},{18,... | collective-permute-start | bytes 1572872 | tf_op jit(solution)/shard_map/ppermute | solution.py:251
where the time goes:
time: 101 us; the launch traced here: 100 us
  starting transfers between devices  30.3 us (30%)
  Pallas kernels  30.2 us (30%)
  waiting for transfers between devices  29.9 us (30%)
  other arithmetic  5.5 us (5%)
  local copies, waits for them, and re-layouts  2.77 us (3%)
  between operations  1.54 us (2%)
    pallas_call x4, Pallas kernels, expert_call(): pl.pallas_call(functools.partial(expert_kernel, slot), in_specs=[anywhere...  22.6 us
    ppermute x7, waiting for transfers between devices, dense_shards(): lax.ppermute(v, 'ep', [(i, i ^ 2) for i in range(experts)])  14.6 us
    ppermute x7, starting transfers between devices, dense_shards(): lax.ppermute(v, 'ep', [(4 * places[n] + i, 4 * places[(n + 1) % ring] + i...  12.9 us
    ppermute x7, starting transfers between devices, dense_shards(): lax.ppermute(v, 'ep', [(i, i ^ 2) for i in range(experts)])  9.03 us
    ppermute x7, waiting for transfers between devices, dense_shards(): lax.ppermute(v, 'ep', [(4 * places[n] + i, 4 * places[(n + 1) % ring] + i...  7.76 us
    all_to_all x1, waiting for transfers between devices, dense_shards(): lax.all_to_all(sent_gates, 'ep', split_axis=0, concat_axis=0, tiled=True,...  7.57 us
    pallas_call x2, Pallas kernels, load(): pl.pallas_call(functools.partial(load_kernel, len(arrays)), in_specs=[pl....  7.56 us
    all_to_all x1, starting transfers between devices, dense_shards(): lax.all_to_all(jnp.broadcast_to(told, (experts * groups, told.shape[1])),...  4.01 us
  transfers between devices with their start and end apart: 19, of which 9 were waited for; matrix products, arithmetic and copies ran while one was open for 7% of the time, Pallas kernels for 30%

commit v1 on v0

--- a/solution.py
+++ b/solution.py
@@ -126,7 +126,7 @@
     )
     for n in range(2):
         for e in range(2):
-            row = gate[pl.ds(2 * slot + n, 1), pl.ds(e * tok, tok)]
+            row = gate[2 * slot + n, pl.ds(e, 1), :]
             scale[e, blocks[n], :] = jnp.sum(
                 jnp.where(diagonal, row, 0.0), axis=1, keepdims=True
             )
@@ -157,6 +157,16 @@
             totals[p] += jnp.sum(lanes[p * PASSAGE : (p + 1) * PASSAGE], axis=0, keepdims=True)
     for p in range(2 * local):
         score[pl.ds(p, 1), :] = totals[p]
+
+
+def gate_kernel(wanted, routes, gates, out):
+    found = jnp.zeros((wanted.shape[0], routes.shape[1]), jnp.float32)
+    values = gates[...].astype(jnp.float32)
+    for k in range(routes.shape[0]):
+        chosen = wanted[...] == routes[pl.ds(k, 1), :]
+        found = jnp.where(chosen, values[k : k + 1], found)
+    for n in range(out.shape[0]):
+        out[n] = found[2 * n : 2 * n + 2].astype(jnp.bfloat16)
 
 
 def load_kernel(count, *refs):
@@ -256,9 +266,12 @@
     cores = [[2 * n + core for n in range(experts // 2)] for core in range(2)]
     target = jnp.arange(experts, dtype=jnp.int32)
     wanted = (target // 2 * 2 + me % 2) ^ target % 2
-    chosen = routes.T[:, None, :] == wanted[None, :, None]
-    sent_gates = jnp.where(chosen, gates.T[:, None, :], jnp.bfloat16(0)).sum(axis=0)
-    sent_gates = sent_gates.reshape(experts // 2, 2 * tok_dev)
+    sent_gates = pl.pallas_call(
+        gate_kernel,
+        out_shape=jax.ShapeDtypeStruct((experts // 2, 2, tok_dev), jnp.bfloat16),
+        compiler_params=pltpu.CompilerParams(vmem_limit_bytes=2**22),
+        name="gates",
+    )(wanted[:, None], routes.T, gates.T)
     gate_rows = lax.all_to_all(
         sent_gates, "ep", split_axis=0, concat_axis=0, tiled=True, axis_index_groups=cores
     )

time: 101 us -> 101 us (level)
  other arithmetic: 5.5 us -> 4.05 us
  transfers between devices with their start and end apart: 19 -> 19, of which waited for: 9 -> 9; matrix products, arithmetic and copies ran while one was open for 7% -> 5% of each run, Pallas kernels for 30% -> 31%
where the time goes in v1:
time: 101 us; the launch traced here: 100 us
  Pallas kernels  30.9 us (31%)
  waiting for transfers between devices  30.4 us (30%)
  starting transfers between devices  30.3 us (30%)
  other arithmetic  4.05 us (4%)
  local copies, waits for them, and re-layouts  3.01 us (3%)
  between operations  1.54 us (2%)
    pallas_call x4, Pallas kernels, expert_call(): pl.pallas_call(functools.partial(expert_kernel, slot), in_specs=[anywhere...  22.6 us
    ppermute x7, waiting for transfers between devices, dense_shards(): lax.ppermute(v, 'ep', [(i, i ^ 2) for i in range(experts)])  14.6 us
    ppermute x7, starting transfers between devices, dense_shards(): lax.ppermute(v, 'ep', [(4 * places[n] + i, 4 * places[(n + 1) % ring] + i...  13 us
    ppermute x7, starting transfers between devices, dense_shards(): lax.ppermute(v, 'ep', [(i, i ^ 2) for i in range(experts)])  9.02 us
    all_to_all x1, waiting for transfers between devices, dense_shards(): lax.all_to_all(sent_gates, 'ep', split_axis=0, concat_axis=0, tiled=True,...  8.1 us
    ppermute x7, waiting for transfers between devices, dense_shards(): lax.ppermute(v, 'ep', [(4 * places[n] + i, 4 * places[(n + 1) % ring] + i...  7.77 us
    pallas_call x2, Pallas kernels, load(): pl.pallas_call(functools.partial(load_kernel, len(arrays)), in_specs=[pl....  7.56 us
    all_to_all x1, starting transfers between devices, dense_shards(): lax.all_to_all(jnp.broadcast_to(told, (experts * groups, told.shape[1])),...  4.01 us
  transfers between devices with their start and end apart: 19, of which 9 were waited for; matrix products, arithmetic and copies ran while one was open for 5% of the time, Pallas kernels for 31%

profile of v1, /device:TPU:0, one launch (start us, length us, event | category | flops | bytes accessed | tf_op | source)
XLA Modules:
  0.0 100.2 jit_solution(16531436139105371239)
XLA Ops:
  1.7 2.6 %collective-permute-start = (bf16[128,2048]{1,0:T(8,128)(2,1)}, bf16[128,2048]{1,0:T(8,128)(2,1)S(1)}, u32[]{:S(2)}, u32[]{:S(2)}) collective-permute-start(bf16[128,2048]{1,0:T(8,128)(2,1)} %xa.1), channel_id=1, source_target_pairs={{0,4},{2,6},{4,0},{6,2},{8,12},{10,14},{12,8},{14,10},{16,20},{18,... | collective-permute-start | bytes 1572872 | tf_op jit(solution)/shard_map/ppermute | solution.py:261
  4.2 2.6 %collective-permute-start.4 = (bf16[128,2048]{1,0:T(8,128)(2,1)}, bf16[128,2048]{1,0:T(8,128)(2,1)S(1)}, u32[]{:S(2)}, u32[]{:S(2)}) collective-permute-start(bf16[128,2048]{1,0:T(8,128)(2,1)} %xa.1), channel_id=1, source_target_pairs={{0,16},{2,18},{4,20},{6,22},{16,24},{18,26},{20,28},{22,30},{24,8}... | collective-permute-start | bytes 1572872 | tf_op jit(solution)/shard_map/ppermute | solution.py:252
  8.9 3.3 %all-to-all-start = ((bf16[8,2,128]{2,1,0:T(2,128)(2,1)}), bf16[8,2,128]{2,1,0:T(2,128)(2,1)S(1)}, u32[]{:S(2)}, u32[]{:S(2)}) async-start(bf16[8,2,128]{2,1,0:T(2,128)(2,1)} %gates.1), calls=%async_computation | async-start | bytes 8192 | tf_op jit(solution)/shard_map/all_to_all | solution.py:275
  12.3 8.1 %all-to-all-done = bf16[8,2,128]{2,1,0:T(2,128)(2,1)S(1)} async-done(((bf16[8,2,128]{2,1,0:T(2,128)(2,1)}), bf16[8,2,128]{2,1,0:T(2,128)(2,1)S(1)}, u32[]{:S(2)}, u32[]{:S(2)}) %all-to-all-start) | async-done | bytes 4128 | tf_op jit(solution)/shard_map/all_to_all | solution.py:275
  21.0 1.7 %collective-permute-start.6 = (bf16[128,2048]{1,0:T(8,128)(2,1)S(1)}, bf16[128,2048]{1,0:T(8,128)(2,1)S(1)}, u32[]{:S(2)}, u32[]{:S(2)}) collective-permute-start(bf16[128,2048]{1,0:T(8,128)(2,1)S(1)} %tie.5.xa), channel_id=1, source_target_pairs={{0,16},{2,18},{4,20},{6,22},{16,24},{18,26},{20,28},{22,30},{24,8}... | collective-permute-start | bytes 1572872 | tf_op jit(solution)/shard_map/ppermute | solution.py:252
  22.7 1.4 %collective-permute-start.5 = (bf16[128,2048]{1,0:T(8,128)(2,1)S(1)}, bf16[128,2048]{1,0:T(8,128)(2,1)S(1)}, u32[]{:S(2)}, u32[]{:S(2)}) collective-permute-start(bf16[128,2048]{1,0:T(8,128)(2,1)S(1)} %tie.5.xa), channel_id=1, source_target_pairs={{0,4},{2,6},{4,0},{6,2},{8,12},{10,14},{12,8},{14,10},{16,20},{18,... | collective-permute-start | bytes 1572872 | tf_op jit(solution)/shard_map/ppermute | solution.py:261
  24.1 3.8 %load.2 = (bf16[2048,768]{1,0:T(8,128)(2,1)S(1)}, bf16[2048,768]{1,0:T(8,128)(2,1)S(1)}, bf16[768,2048]{1,0:T(8,128)(2,1)S(1)}) custom-call(f32[8,2,128]{2,1,0:T(2,128)S(1)} %gather_fusion, bf16[2048,768]{1,0:T(8,128)(2,1)} %bitcast.38, bf16[2048,768]{1,0:T(8,128)(2,1)} %bitcast.40, bf16[768,2048]{1,0:T(8,128)(2,1)} %bitcast.42), custom_call_target="tpu_custom_call" | custom-call | tf_op jit(solution)/shard_map/load/pallas_call | solution.py:186
  27.9 6.1 %collective-permute-done.6.refs_2_ = bf16[128,2048]{1,0:T(8,128)(2,1)S(1)} collective-permute-done((bf16[128,2048]{1,0:T(8,128)(2,1)S(1)}, bf16[128,2048]{1,0:T(8,128)(2,1)S(1)}, u32[]{:S(2)}, u32[]{:S(2)}) %collective-permute-start.6) | collective-permute-done | bytes 524320 | tf_op jit(solution)/shard_map/ppermute | solution.py:252
  34.0 1.5 %collective-permute-done.5.refs_0_.xb = bf16[128,2048]{1,0:T(8,128)(2,1)S(1)} collective-permute-done((bf16[128,2048]{1,0:T(8,128)(2,1)S(1)}, bf16[128,2048]{1,0:T(8,128)(2,1)S(1)}, u32[]{:S(2)}, u32[]{:S(2)}) %collective-permute-start.5) | collective-permute-done | bytes 524320 | tf_op jit(solution)/shard_map/ppermute | solution.py:261
  36.7 1.4 %collective-permute-start.7 = (bf16[128,2048]{1,0:T(8,128)(2,1)S(1)}, bf16[128,2048]{1,0:T(8,128)(2,1)S(1)}, u32[]{:S(2)}, u32[]{:S(2)}) collective-permute-start(bf16[128,2048]{1,0:T(8,128)(2,1)S(1)} %tie.6.after.xa), channel_id=1, source_target_pairs={{0,4},{2,6},{4,0},{6,2},{8,12},{10,14},{12,8},{14,10},{16,20},{18,... | collective-permute-start | bytes 1572872 | tf_op jit(solution)/shard_map/ppermute | solution.py:261
  38.1 3.8 %load.3 = (bf16[2048,768]{1,0:T(8,128)(2,1)S(1)}, bf16[2048,768]{1,0:T(8,128)(2,1)S(1)}, bf16[768,2048]{1,0:T(8,128)(2,1)S(1)}) custom-call(f32[8,2,128]{2,1,0:T(2,128)S(1)} %gather_fusion, bf16[2048,768]{1,0:T(8,128)(2,1)} %collective-permute-done.1.refs_1_, bf16[2048,768]{1,0:T(8,128)(2,1)} %collective-permute-done.2.refs_2_, ...), custom_call_target="tpu_custom_call" | custom-call | tf_op jit(solution)/shard_map/load/pallas_call | solution.py:186
  42.0 5.7 %expert.4 = (bf16[128,2048]{1,0:T(8,128)(2,1)S(1)}, bf16[128,2048]{1,0:T(8,128)(2,1)S(1)}, f32[2,128]{1,0:T(2,128)S(1)}, f32[8,128]{1,0:T(8,128)S(1)}) custom-call(bf16[128,2048]{1,0:T(8,128)(2,1)S(1)} %tie.5.xa, bf16[128,2048]{1,0:T(8,128)(2,1)S(1)} %collective-permute-done.5.refs_0_.xb, ...), custom_call_target="tpu_custom_call", output_to_operand_aliasing={{3}: (11, {})} | custom-call | flops 1 | bytes 1 | tf_op jit(solution)/shard_map/expert/pallas_call | solution.py:221
  50.0 5.7 %expert.5 = (bf16[128,2048]{1,0:T(8,128)(2,1)S(1)}, bf16[128,2048]{1,0:T(8,128)(2,1)S(1)}, f32[2,128]{1,0:T(2,128)S(1)}, f32[8,128]{1,0:T(8,128)S(1)}) custom-call(bf16[128,2048]{1,0:T(8,128)(2,1)S(1)} %copy-done, bf16[128,2048]{1,0:T(8,128)(2,1)S(1)} %collective-permute-done.refs_0_.xb, ...), custom_call_target="tpu_custom_call", output_to_operand_aliasing={{3}: (11, {})} | custom-call | flops 1 | bytes 1 | tf_op jit(solution)/shard_map/expert/pallas_call | solution.py:221
  55.6 5.7 %expert.6 = (bf16[128,2048]{1,0:T(8,128)(2,1)S(1)}, bf16[128,2048]{1,0:T(8,128)(2,1)S(1)}, f32[2,128]{1,0:T(2,128)S(1)}, f32[8,128]{1,0:T(8,128)S(1)}) custom-call(bf16[128,2048]{1,0:T(8,128)(2,1)S(1)} %tie.6.after.xa, bf16[128,2048]{1,0:T(8,128)(2,1)S(1)} %collective-permute-done.7.refs_0_.xb, ...), custom_call_target="tpu_custom_call", output_to_operand_aliasing={{3}: (11, {})} | custom-call | flops 1 | bytes 1 | tf_op jit(solution)/shard_map/expert/pallas_call | solution.py:221
  61.3 1.2 %collective-permute-start.11 = (bf16[128,2048]{1,0:T(8,128)(2,1)S(1)}, bf16[128,2048]{1,0:T(8,128)(2,1)S(1)}, u32[]{:S(2)}, u32[]{:S(2)}) collective-permute-start(bf16[128,2048]{1,0:T(8,128)(2,1)S(1)} %get-tuple-element.39), channel_id=1, source_target_pairs={{0,4},{2,6},{4,0},{6,2},{8,12},{10,14},{12,8},{14,10},{16,20},{18,... | collective-permute-start | bytes 1572872 | tf_op jit(solution)/shard_map/ppermute | solution.py:261
  62.6 1.7 %collective-permute-start.13 = (bf16[128,2048]{1,0:T(8,128)(2,1)S(1)}, bf16[128,2048]{1,0:T(8,128)(2,1)S(1)}, u32[]{:S(2)}, u32[]{:S(2)}) collective-permute-start(bf16[128,2048]{1,0:T(8,128)(2,1)S(1)} %add_convert_fusion.3), channel_id=1, source_target_pairs={{0,16},{2,18},{4,20},{6,22},{16,24},{18,26},{20,28},{22,30},{24,8}... | collective-permute-start | bytes 1572872 | tf_op jit(solution)/shard_map/ppermute | solution.py:252
  65.0 5.7 %expert.7 = (bf16[128,2048]{1,0:T(8,128)(2,1)S(1)}, bf16[128,2048]{1,0:T(8,128)(2,1)S(1)}, f32[2,128]{1,0:T(2,128)S(1)}, bf16[128,2048]{1,0:T(8,128)(2,1)S(1)}) custom-call(bf16[128,2048]{1,0:T(8,128)(2,1)S(1)} %tie.7.after.xa, bf16[128,2048]{1,0:T(8,128)(2,1)S(1)} %collective-permute-done.9.xb, ...), custom_call_target="tpu_custom_call", output_to_operand_aliasing={{3}: (11, {})} | custom-call | flops 1 | bytes 1 | tf_op jit(solution)/shard_map/expert/pallas_call | solution.py:221
  71.7 2.1 %collective-permute-done.11 = bf16[128,2048]{1,0:T(8,128)(2,1)S(1)} collective-permute-done((bf16[128,2048]{1,0:T(8,128)(2,1)S(1)}, bf16[128,2048]{1,0:T(8,128)(2,1)S(1)}, u32[]{:S(2)}, u32[]{:S(2)}) %collective-permute-start.11) | collective-permute-done | bytes 524320 | tf_op jit(solution)/shard_map/ppermute | solution.py:261
  74.4 2.1 %collective-permute-start.14 = (bf16[128,2048]{1,0:T(8,128)(2,1)S(1)}, bf16[128,2048]{1,0:T(8,128)(2,1)}, u32[]{:S(2)}, u32[]{:S(2)}) collective-permute-start(bf16[128,2048]{1,0:T(8,128)(2,1)S(1)} %add_convert_fusion.2.refs_0_), channel_id=1, source_target_pairs={{0,16},{2,18},{4,20},{6,22},{16,24},{18,26},{20,28},{22,30},{24,8}... | collective-permute-start | bytes 1572872 | tf_op jit(solution)/shard_map/ppermute | solution.py:252
  77.4 4.0 %all-to-all-start.1 = ((f32[32,1,128]{2,1,0:T(1,128)}), f32[32,1,128]{2,1,0:T(1,128)S(1)}, u32[]{:S(2)}, u32[]{:S(2)}) async-start(f32[32,1,128]{2,1,0:T(1,128)} %broadcast_in_dim.74), calls=%async_computation.1 | async-start | bytes 32768 | tf_op jit(solution)/shard_map/all_to_all | solution.py:342
  82.6 1.3 %collective-permute-done.14 = bf16[128,2048]{1,0:T(8,128)(2,1)} collective-permute-done((bf16[128,2048]{1,0:T(8,128)(2,1)S(1)}, bf16[128,2048]{1,0:T(8,128)(2,1)}, u32[]{:S(2)}, u32[]{:S(2)}) %collective-permute-start.14) | collective-permute-done | bytes 524320 | tf_op jit(solution)/shard_map/ppermute | solution.py:252
  83.8 1.3 %add_convert_fusion.1.refs_0_ = bf16[128,2048]{1,0:T(8,128)(2,1)S(1)} fusion(bf16[128,2048]{1,0:T(8,128)(2,1)} %collective-permute-done.14, bf16[128,2048]{1,0:T(8,128)(2,1)S(1)} %collective-permute-done.10, bf16[128,2048]{1,0:T(8,128)(2,1)S(1)} %get-tuple-element.36), kind=kLoop, calls=%fused_computation.2 | loop fusion | flops 1572864 | bytes 2097152 | tf_op jit(solution)/shard_map/convert_element_type | solution.py:331
  85.1 3.1 %collective-permute-start.16 = (bf16[128,2048]{1,0:T(8,128)(2,1)S(1)}, bf16[128,2048]{1,0:T(8,128)(2,1)S(1)}, u32[]{:S(2)}, u32[]{:S(2)}) collective-permute-start(bf16[128,2048]{1,0:T(8,128)(2,1)S(1)} %add_convert_fusion.1.refs_0_), channel_id=1, source_target_pairs={{0,16},{2,18},{4,20},{6,22},{16,24},{18,26},{20,28},{22,30},{24,8}... | collective-permute-start | bytes 1572872 | tf_op jit(solution)/shard_map/ppermute | solution.py:252
  90.4 8.8 %collective-permute-done.15 = bf16[128,2048]{1,0:T(8,128)(2,1)S(1)} collective-permute-done((bf16[128,2048]{1,0:T(8,128)(2,1)S(1)}, bf16[128,2048]{1,0:T(8,128)(2,1)S(1)}, u32[]{:S(2)}, u32[]{:S(2)}) %collective-permute-start.15) | collective-permute-done | bytes 524320 | tf_op jit(solution)/shard_map/ppermute | solution.py:261
  (59 shorter events, 14.3 us)
Async XLA Ops:
  0.6 37.5 %collective-permute-start.1 = (bf16[2048,768]{1,0:T(8,128)(2,1)}, bf16[2048,768]{1,0:T(8,128)(2,1)}, u32[]{:S(2)}, u32[]{:S(2)}) collective-permute-start(bf16[2048,768]{1,0:T(8,128)(2,1)} %bitcast.37), channel_id=1, source_target_pairs={{0,2},{2,0},{4,6},{6,4},{8,10},{10,8},{12,14},{14,12},{16,18},{18,... | collective-permute-start | bytes 9437192 | tf_op jit(solution)/shard_map/ppermute | solution.py:262
  1.1 37.0 %collective-permute-start.2 = (bf16[2048,768]{1,0:T(8,128)(2,1)}, bf16[2048,768]{1,0:T(8,128)(2,1)}, u32[]{:S(2)}, u32[]{:S(2)}) collective-permute-start(bf16[2048,768]{1,0:T(8,128)(2,1)} %bitcast.39), channel_id=1, source_target_pairs={{0,2},{2,0},{4,6},{6,4},{8,10},{10,8},{12,14},{14,12},{16,18},{18,... | collective-permute-start | bytes 9437192 | tf_op jit(solution)/shard_map/ppermute | solution.py:262
  1.2 36.9 %collective-permute-start.3 = (bf16[768,2048]{1,0:T(8,128)(2,1)}, bf16[768,2048]{1,0:T(8,128)(2,1)}, u32[]{:S(2)}, u32[]{:S(2)}) collective-permute-start(bf16[768,2048]{1,0:T(8,128)(2,1)} %bitcast.41), channel_id=1, source_target_pairs={{0,2},{2,0},{4,6},{6,4},{8,10},{10,8},{12,14},{14,12},{16,18},{18,... | collective-permute-start | bytes 9437192 | tf_op jit(solution)/shard_map/ppermute | solution.py:262
  1.7 19.3 %collective-permute-start = (bf16[128,2048]{1,0:T(8,128)(2,1)}, bf16[128,2048]{1,0:T(8,128)(2,1)S(1)}, u32[]{:S(2)}, u32[]{:S(2)}) collective-permute-start(bf16[128,2048]{1,0:T(8,128)(2,1)} %xa.1), channel_id=1, source_target_pairs={{0,4},{2,6},{4,0},{6,2},{8,12},{10,14},{12,8},{14,10},{16,20},{18,... | collective-permute-start | bytes 1572872 | tf_op jit(solution)/shard_map/ppermute | solution.py:261
  4.2 16.8 %collective-permute-start.4 = (bf16[128,2048]{1,0:T(8,128)(2,1)}, bf16[128,2048]{1,0:T(8,128)(2,1)S(1)}, u32[]{:S(2)}, u32[]{:S(2)}) collective-permute-start(bf16[128,2048]{1,0:T(8,128)(2,1)} %xa.1), channel_id=1, source_target_pairs={{0,16},{2,18},{4,20},{6,22},{16,24},{18,26},{20,28},{22,30},{24,8}... | collective-permute-start | bytes 1572872 | tf_op jit(solution)/shard_map/ppermute | solution.py:252
  6.8 0.7 copy-start.2
  7.5 0.7 copy-start.3
  8.9 11.5 %all-to-all-start = ((bf16[8,2,128]{2,1,0:T(2,128)(2,1)}), bf16[8,2,128]{2,1,0:T(2,128)(2,1)S(1)}, u32[]{:S(2)}, u32[]{:S(2)}) async-start(bf16[8,2,128]{2,1,0:T(2,128)(2,1)} %gates.1), calls=%async_computation | async-start | bytes 8192 | tf_op jit(solution)/shard_map/all_to_all | solution.py:275
  21.0 12.9 %collective-permute-start.6 = (bf16[128,2048]{1,0:T(8,128)(2,1)S(1)}, bf16[128,2048]{1,0:T(8,128)(2,1)S(1)}, u32[]{:S(2)}, u32[]{:S(2)}) collective-permute-start(bf16[128,2048]{1,0:T(8,128)(2,1)S(1)} %tie.5.xa), channel_id=1, source_target_pairs={{0,16},{2,18},{4,20},{6,22},{16,24},{18,26},{20,28},{22,30},{24,8}... | collective-permute-start | bytes 1572872 | tf_op jit(solution)/shard_map/ppermute | solution.py:252
  22.7 12.8 %collective-permute-start.5 = (bf16[128,2048]{1,0:T(8,128)(2,1)S(1)}, bf16[128,2048]{1,0:T(8,128)(2,1)S(1)}, u32[]{:S(2)}, u32[]{:S(2)}) collective-permute-start(bf16[128,2048]{1,0:T(8,128)(2,1)S(1)} %tie.5.xa), channel_id=1, source_target_pairs={{0,4},{2,6},{4,0},{6,2},{8,12},{10,14},{12,8},{14,10},{16,20},{18,... | collective-permute-start | bytes 1572872 | tf_op jit(solution)/shard_map/ppermute | solution.py:261
  35.5 6.4 %copy-start.1 = (f32[2048]{0:T(1024)S(1)}, f32[2048]{0:T(1024)}, u32[]{:S(2)}) copy-start(f32[2048]{0:T(1024)} %param.14) | copy-start | bytes 24580
  35.5 14.5 %collective-permute-start.8 = (bf16[128,2048]{1,0:T(8,128)(2,1)S(1)}, bf16[128,2048]{1,0:T(8,128)(2,1)S(1)}, u32[]{:S(2)}, u32[]{:S(2)}) collective-permute-start(bf16[128,2048]{1,0:T(8,128)(2,1)S(1)} %tie.6.after.xa), channel_id=1, source_target_pairs={{0,16},{2,18},{4,20},{6,22},{16,24},{18,26},{20,28},{22,30},{24,8}... | collective-permute-start | bytes 1572872 | tf_op jit(solution)/shard_map/ppermute | solution.py:252
  36.7 12.7 %collective-permute-start.7 = (bf16[128,2048]{1,0:T(8,128)(2,1)S(1)}, bf16[128,2048]{1,0:T(8,128)(2,1)S(1)}, u32[]{:S(2)}, u32[]{:S(2)}) collective-permute-start(bf16[128,2048]{1,0:T(8,128)(2,1)S(1)} %tie.6.after.xa), channel_id=1, source_target_pairs={{0,4},{2,6},{4,0},{6,2},{8,12},{10,14},{12,8},{14,10},{16,20},{18,... | collective-permute-start | bytes 1572872 | tf_op jit(solution)/shard_map/ppermute | solution.py:261
  41.9 8.0 %copy-start = (bf16[128,2048]{1,0:T(8,128)(2,1)S(1)}, bf16[128,2048]{1,0:T(8,128)(2,1)}, u32[]{:S(2)}) copy-start(bf16[128,2048]{1,0:T(8,128)(2,1)} %xa.1) | copy-start | bytes 1572868
  47.6 14.9 %collective-permute-start.12 = (bf16[128,2048]{1,0:T(8,128)(2,1)S(1)}, bf16[128,2048]{1,0:T(8,128)(2,1)S(1)}, u32[]{:S(2)}, u32[]{:S(2)}) collective-permute-start(bf16[128,2048]{1,0:T(8,128)(2,1)S(1)} %get-tuple-element.41), channel_id=1, source_target_pairs={{0,4},{2,6},{4,0},{6,2},{8,12},{10,14},{12,8},{14,10},{16,20},{18,... | collective-permute-start | bytes 1572872 | tf_op jit(solution)/shard_map/ppermute | solution.py:261
  49.4 15.6 %collective-permute-start.9 = (bf16[128,2048]{1,0:T(8,128)(2,1)S(1)}, bf16[128,2048]{1,0:T(8,128)(2,1)S(1)}, u32[]{:S(2)}, u32[]{:S(2)}) collective-permute-start(bf16[128,2048]{1,0:T(8,128)(2,1)S(1)} %collective-permute-done.7.refs_0_.xb), channel_id=1, source_target_pairs={{0,16},{2,18},{4,20},{6,22},{16,24},{18,26},{20,28},{22,30},{24,8}... | collective-permute-start | bytes 1572872 | tf_op jit(solution)/shard_map/ppermute | solution.py:252
  61.3 12.4 %collective-permute-start.11 = (bf16[128,2048]{1,0:T(8,128)(2,1)S(1)}, bf16[128,2048]{1,0:T(8,128)(2,1)S(1)}, u32[]{:S(2)}, u32[]{:S(2)}) collective-permute-start(bf16[128,2048]{1,0:T(8,128)(2,1)S(1)} %get-tuple-element.39), channel_id=1, source_target_pairs={{0,4},{2,6},{4,0},{6,2},{8,12},{10,14},{12,8},{14,10},{16,20},{18,... | collective-permute-start | bytes 1572872 | tf_op jit(solution)/shard_map/ppermute | solution.py:261
  62.6 11.5 %collective-permute-start.13 = (bf16[128,2048]{1,0:T(8,128)(2,1)S(1)}, bf16[128,2048]{1,0:T(8,128)(2,1)S(1)}, u32[]{:S(2)}, u32[]{:S(2)}) collective-permute-start(bf16[128,2048]{1,0:T(8,128)(2,1)S(1)} %add_convert_fusion.3), channel_id=1, source_target_pairs={{0,16},{2,18},{4,20},{6,22},{16,24},{18,26},{20,28},{22,30},{24,8}... | collective-permute-start | bytes 1572872 | tf_op jit(solution)/shard_map/ppermute | solution.py:252
  70.7 11.8 %collective-permute-start.10 = (bf16[128,2048]{1,0:T(8,128)(2,1)S(1)}, bf16[128,2048]{1,0:T(8,128)(2,1)S(1)}, u32[]{:S(2)}, u32[]{:S(2)}) collective-permute-start(bf16[128,2048]{1,0:T(8,128)(2,1)S(1)} %get-tuple-element.37), channel_id=1, source_target_pairs={{0,4},{2,6},{4,0},{6,2},{8,12},{10,14},{12,8},{14,10},{16,20},{18,... | collective-permute-start | bytes 1572872 | tf_op jit(solution)/shard_map/ppermute | solution.py:261
  74.4 9.4 %collective-permute-start.14 = (bf16[128,2048]{1,0:T(8,128)(2,1)S(1)}, bf16[128,2048]{1,0:T(8,128)(2,1)}, u32[]{:S(2)}, u32[]{:S(2)}) collective-permute-start(bf16[128,2048]{1,0:T(8,128)(2,1)S(1)} %add_convert_fusion.2.refs_0_), channel_id=1, source_target_pairs={{0,16},{2,18},{4,20},{6,22},{16,24},{18,26},{20,28},{22,30},{24,8}... | collective-permute-start | bytes 1572872 | tf_op jit(solution)/shard_map/ppermute | solution.py:252
  77.4 11.6 %all-to-all-start.1 = ((f32[32,1,128]{2,1,0:T(1,128)}), f32[32,1,128]{2,1,0:T(1,128)S(1)}, u32[]{:S(2)}, u32[]{:S(2)}) async-start(f32[32,1,128]{2,1,0:T(1,128)} %broadcast_in_dim.74), calls=%async_computation.1 | async-start | bytes 32768 | tf_op jit(solution)/shard_map/all_to_all | solution.py:342
  85.1 14.1 %collective-permute-start.16 = (bf16[128,2048]{1,0:T(8,128)(2,1)S(1)}, bf16[128,2048]{1,0:T(8,128)(2,1)S(1)}, u32[]{:S(2)}, u32[]{:S(2)}) collective-permute-start(bf16[128,2048]{1,0:T(8,128)(2,1)S(1)} %add_convert_fusion.1.refs_0_), channel_id=1, source_target_pairs={{0,16},{2,18},{4,20},{6,22},{16,24},{18,26},{20,28},{22,30},{24,8}... | collective-permute-start | bytes 1572872 | tf_op jit(solution)/shard_map/ppermute | solution.py:252
  88.2 11.0 %collective-permute-start.15 = (bf16[128,2048]{1,0:T(8,128)(2,1)S(1)}, bf16[128,2048]{1,0:T(8,128)(2,1)S(1)}, u32[]{:S(2)}, u32[]{:S(2)}) collective-permute-start(bf16[128,2048]{1,0:T(8,128)(2,1)S(1)} %tie.8), channel_id=1, source_target_pairs={{0,4},{2,6},{4,0},{6,2},{8,12},{10,14},{12,8},{14,10},{16,20},{18,... | collective-permute-start | bytes 1572872 | tf_op jit(solution)/shard_map/ppermute | solution.py:261

commit v2 on v0

--- a/solution.py
+++ b/solution.py
@@ -311,11 +311,13 @@
     carried = None
     sent = []
     for s in [*range(1, ring), 0]:
-        crossing = tie(other[0], sent[-1]) if s == 0 else other[s]
-        total = mine[s].astype(jnp.float32) + across(crossing).astype(jnp.float32)
+        total = mine[s].astype(jnp.float32) + across(other[s]).astype(jnp.float32)
         if carried is not None:
             total = total + carried.astype(jnp.float32)
         total = total.astype(jnp.bfloat16)
+        if s == ring - 1:
+            other[0] = tie(other[0], total)
+            total = tie(total, other[0])
         if s > 0:
             carried = onward(total)
             sent.append(total)

time: 101 us -> 99.7 us (0.987)
    ppermute x7, waiting for transfers between devices: 14.6 us -> 5.81 us  [dense_shards(): lax.ppermute(v, 'ep', [(i, i ^ 2) for i in range(experts)])]
    ppermute x7, waiting for transfers between devices: 7.76 us -> 15.6 us  [dense_shards(): lax.ppermute(v, 'ep', [(4 * places[n] + i, 4 * places[(n + 1) % ring] + i...]
where the time goes in v2:
time: 99.7 us; the launch traced here: 99.4 us
  starting transfers between devices  30.3 us (30%)
  Pallas kernels  30.2 us (30%)
  waiting for transfers between devices  29 us (29%)
  other arithmetic  5.5 us (6%)
  local copies, waits for them, and re-layouts  2.77 us (3%)
  between operations  1.56 us (2%)
    pallas_call x4, Pallas kernels, expert_call(): pl.pallas_call(functools.partial(expert_kernel, slot), in_specs=[anywhere...  22.6 us
    ppermute x7, waiting for transfers between devices, dense_shards(): lax.ppermute(v, 'ep', [(4 * places[n] + i, 4 * places[(n + 1) % ring] + i...  15.6 us
    ppermute x7, starting transfers between devices, dense_shards(): lax.ppermute(v, 'ep', [(4 * places[n] + i, 4 * places[(n + 1) % ring] + i...  12.7 us
    ppermute x7, starting transfers between devices, dense_shards(): lax.ppermute(v, 'ep', [(i, i ^ 2) for i in range(experts)])  9.24 us
    all_to_all x1, waiting for transfers between devices, dense_shards(): lax.all_to_all(sent_gates, 'ep', split_axis=0, concat_axis=0, tiled=True,...  7.57 us
    pallas_call x2, Pallas kernels, load(): pl.pallas_call(functools.partial(load_kernel, len(arrays)), in_specs=[pl....  7.56 us
    ppermute x7, waiting for transfers between devices, dense_shards(): lax.ppermute(v, 'ep', [(i, i ^ 2) for i in range(experts)])  5.81 us
    all_to_all x1, starting transfers between devices, dense_shards(): lax.all_to_all(jnp.broadcast_to(told, (experts * groups, told.shape[1])),...  4.01 us
  transfers between devices with their start and end apart: 19, of which 9 were waited for; matrix products, arithmetic and copies ran while one was open for 7% of the time, Pallas kernels for 30%

profile of v2, /device:TPU:0, one launch (start us, length us, event | category | flops | bytes accessed | tf_op | source)
XLA Modules:
  0.0 99.4 jit_solution(4318058515590807411)
XLA Ops:
  1.7 2.6 %collective-permute-start = (bf16[128,2048]{1,0:T(8,128)(2,1)}, bf16[128,2048]{1,0:T(8,128)(2,1)S(1)}, u32[]{:S(2)}, u32[]{:S(2)}) collective-permute-start(bf16[128,2048]{1,0:T(8,128)(2,1)} %xa.1), channel_id=1, source_target_pairs={{0,4},{2,6},{4,0},{6,2},{8,12},{10,14},{12,8},{14,10},{16,20},{18,... | collective-permute-start | bytes 1572872 | tf_op jit(solution)/shard_map/ppermute | solution.py:251
  4.2 2.6 %collective-permute-start.4 = (bf16[128,2048]{1,0:T(8,128)(2,1)}, bf16[128,2048]{1,0:T(8,128)(2,1)S(1)}, u32[]{:S(2)}, u32[]{:S(2)}) collective-permute-start(bf16[128,2048]{1,0:T(8,128)(2,1)} %xa.1), channel_id=1, source_target_pairs={{0,16},{2,18},{4,20},{6,22},{16,24},{18,26},{20,28},{22,30},{24,8}... | collective-permute-start | bytes 1572872 | tf_op jit(solution)/shard_map/ppermute | solution.py:242
  9.4 3.3 %all-to-all-start = ((bf16[8,2,128]{2,1,0:T(2,128)(2,1)}), bf16[8,2,128]{2,1,0:T(2,128)(2,1)S(1)}, u32[]{:S(2)}, u32[]{:S(2)}) async-start(bf16[8,2,128]{2,1,0:T(2,128)(2,1)} %reshape.293), calls=%async_computation | async-start | bytes 8192 | tf_op jit(solution)/shard_map/all_to_all | solution.py:262
  12.8 7.6 %all-to-all-done = bf16[8,2,128]{2,1,0:T(2,128)(2,1)S(1)} async-done(((bf16[8,2,128]{2,1,0:T(2,128)(2,1)}), bf16[8,2,128]{2,1,0:T(2,128)(2,1)S(1)}, u32[]{:S(2)}, u32[]{:S(2)}) %all-to-all-start) | async-done | bytes 4128 | tf_op jit(solution)/shard_map/all_to_all | solution.py:262
  21.0 1.7 %collective-permute-start.6 = (bf16[128,2048]{1,0:T(8,128)(2,1)S(1)}, bf16[128,2048]{1,0:T(8,128)(2,1)S(1)}, u32[]{:S(2)}, u32[]{:S(2)}) collective-permute-start(bf16[128,2048]{1,0:T(8,128)(2,1)S(1)} %tie.6.xa), channel_id=1, source_target_pairs={{0,16},{2,18},{4,20},{6,22},{16,24},{18,26},{20,28},{22,30},{24,8}... | collective-permute-start | bytes 1572872 | tf_op jit(solution)/shard_map/ppermute | solution.py:242
  22.7 1.4 %collective-permute-start.5 = (bf16[128,2048]{1,0:T(8,128)(2,1)S(1)}, bf16[128,2048]{1,0:T(8,128)(2,1)S(1)}, u32[]{:S(2)}, u32[]{:S(2)}) collective-permute-start(bf16[128,2048]{1,0:T(8,128)(2,1)S(1)} %tie.6.xa), channel_id=1, source_target_pairs={{0,4},{2,6},{4,0},{6,2},{8,12},{10,14},{12,8},{14,10},{16,20},{18,... | collective-permute-start | bytes 1572872 | tf_op jit(solution)/shard_map/ppermute | solution.py:251
  24.1 3.8 %load.2 = (bf16[2048,768]{1,0:T(8,128)(2,1)S(1)}, bf16[2048,768]{1,0:T(8,128)(2,1)S(1)}, bf16[768,2048]{1,0:T(8,128)(2,1)S(1)}) custom-call(f32[8,256]{1,0:T(8,128)S(1)} %gather_fusion, bf16[2048,768]{1,0:T(8,128)(2,1)} %bitcast.39, bf16[2048,768]{1,0:T(8,128)(2,1)} %bitcast.41, bf16[768,2048]{1,0:T(8,128)(2,1)} %bitcast.43), custom_call_target="tpu_custom_call" | custom-call | tf_op jit(solution)/shard_map/load/pallas_call | solution.py:176
  27.9 6.1 %collective-permute-done.6.refs_2_ = bf16[128,2048]{1,0:T(8,128)(2,1)S(1)} collective-permute-done((bf16[128,2048]{1,0:T(8,128)(2,1)S(1)}, bf16[128,2048]{1,0:T(8,128)(2,1)S(1)}, u32[]{:S(2)}, u32[]{:S(2)}) %collective-permute-start.6) | collective-permute-done | bytes 524320 | tf_op jit(solution)/shard_map/ppermute | solution.py:242
  34.0 1.5 %collective-permute-done.5.refs_0_.xb = bf16[128,2048]{1,0:T(8,128)(2,1)S(1)} collective-permute-done((bf16[128,2048]{1,0:T(8,128)(2,1)S(1)}, bf16[128,2048]{1,0:T(8,128)(2,1)S(1)}, u32[]{:S(2)}, u32[]{:S(2)}) %collective-permute-start.5) | collective-permute-done | bytes 524320 | tf_op jit(solution)/shard_map/ppermute | solution.py:251
  36.7 1.4 %collective-permute-start.7 = (bf16[128,2048]{1,0:T(8,128)(2,1)S(1)}, bf16[128,2048]{1,0:T(8,128)(2,1)S(1)}, u32[]{:S(2)}, u32[]{:S(2)}) collective-permute-start(bf16[128,2048]{1,0:T(8,128)(2,1)S(1)} %tie.7.after.xa), channel_id=1, source_target_pairs={{0,4},{2,6},{4,0},{6,2},{8,12},{10,14},{12,8},{14,10},{16,20},{18,... | collective-permute-start | bytes 1572872 | tf_op jit(solution)/shard_map/ppermute | solution.py:251
  38.1 3.8 %load.3 = (bf16[2048,768]{1,0:T(8,128)(2,1)S(1)}, bf16[2048,768]{1,0:T(8,128)(2,1)S(1)}, bf16[768,2048]{1,0:T(8,128)(2,1)S(1)}) custom-call(f32[8,256]{1,0:T(8,128)S(1)} %gather_fusion, bf16[2048,768]{1,0:T(8,128)(2,1)} %collective-permute-done.1.refs_1_, bf16[2048,768]{1,0:T(8,128)(2,1)} %collective-permute-done.2.refs_2_, ...), custom_call_target="tpu_custom_call" | custom-call | tf_op jit(solution)/shard_map/load/pallas_call | solution.py:176
  42.0 5.7 %expert.4 = (bf16[128,2048]{1,0:T(8,128)(2,1)S(1)}, bf16[128,2048]{1,0:T(8,128)(2,1)S(1)}, f32[2,128]{1,0:T(2,128)S(1)}, f32[8,128]{1,0:T(8,128)S(1)}) custom-call(bf16[128,2048]{1,0:T(8,128)(2,1)S(1)} %tie.6.xa, bf16[128,2048]{1,0:T(8,128)(2,1)S(1)} %collective-permute-done.5.refs_0_.xb, ...), custom_call_target="tpu_custom_call", output_to_operand_aliasing={{3}: (11, {})} | custom-call | flops 1 | bytes 1 | tf_op jit(solution)/shard_map/expert/pallas_call | solution.py:211
  50.0 5.7 %expert.5 = (bf16[128,2048]{1,0:T(8,128)(2,1)S(1)}, bf16[128,2048]{1,0:T(8,128)(2,1)S(1)}, f32[2,128]{1,0:T(2,128)S(1)}, f32[8,128]{1,0:T(8,128)S(1)}) custom-call(bf16[128,2048]{1,0:T(8,128)(2,1)S(1)} %copy-done, bf16[128,2048]{1,0:T(8,128)(2,1)S(1)} %collective-permute-done.refs_0_.xb, ...), custom_call_target="tpu_custom_call", output_to_operand_aliasing={{3}: (11, {})} | custom-call | flops 1 | bytes 1 | tf_op jit(solution)/shard_map/expert/pallas_call | solution.py:211
  55.7 5.7 %expert.6 = (bf16[128,2048]{1,0:T(8,128)(2,1)S(1)}, bf16[128,2048]{1,0:T(8,128)(2,1)S(1)}, f32[2,128]{1,0:T(2,128)S(1)}, f32[8,128]{1,0:T(8,128)S(1)}) custom-call(bf16[128,2048]{1,0:T(8,128)(2,1)S(1)} %tie.7.after.xa, bf16[128,2048]{1,0:T(8,128)(2,1)S(1)} %collective-permute-done.7.refs_0_.xb, ...), custom_call_target="tpu_custom_call", output_to_operand_aliasing={{3}: (11, {})} | custom-call | flops 1 | bytes 1 | tf_op jit(solution)/shard_map/expert/pallas_call | solution.py:211
  61.3 1.2 %collective-permute-start.11 = (bf16[128,2048]{1,0:T(8,128)(2,1)S(1)}, bf16[128,2048]{1,0:T(8,128)(2,1)S(1)}, u32[]{:S(2)}, u32[]{:S(2)}) collective-permute-start(bf16[128,2048]{1,0:T(8,128)(2,1)S(1)} %get-tuple-element.39), channel_id=1, source_target_pairs={{0,4},{2,6},{4,0},{6,2},{8,12},{10,14},{12,8},{14,10},{16,20},{18,... | collective-permute-start | bytes 1572872 | tf_op jit(solution)/shard_map/ppermute | solution.py:251
  62.6 1.7 %collective-permute-start.13 = (bf16[128,2048]{1,0:T(8,128)(2,1)S(1)}, bf16[128,2048]{1,0:T(8,128)(2,1)S(1)}, u32[]{:S(2)}, u32[]{:S(2)}) collective-permute-start(bf16[128,2048]{1,0:T(8,128)(2,1)S(1)} %add_convert_fusion.3), channel_id=1, source_target_pairs={{0,16},{2,18},{4,20},{6,22},{16,24},{18,26},{20,28},{22,30},{24,8}... | collective-permute-start | bytes 1572872 | tf_op jit(solution)/shard_map/ppermute | solution.py:242
  65.0 5.7 %expert.7 = (bf16[128,2048]{1,0:T(8,128)(2,1)S(1)}, bf16[128,2048]{1,0:T(8,128)(2,1)S(1)}, f32[2,128]{1,0:T(2,128)S(1)}, bf16[128,2048]{1,0:T(8,128)(2,1)S(1)}) custom-call(bf16[128,2048]{1,0:T(8,128)(2,1)S(1)} %tie.8.after.xa, bf16[128,2048]{1,0:T(8,128)(2,1)S(1)} %collective-permute-done.9.xb, ...), custom_call_target="tpu_custom_call", output_to_operand_aliasing={{3}: (11, {})} | custom-call | flops 1 | bytes 1 | tf_op jit(solution)/shard_map/expert/pallas_call | solution.py:211
  71.7 2.1 %collective-permute-done.11 = bf16[128,2048]{1,0:T(8,128)(2,1)S(1)} collective-permute-done((bf16[128,2048]{1,0:T(8,128)(2,1)S(1)}, bf16[128,2048]{1,0:T(8,128)(2,1)S(1)}, u32[]{:S(2)}, u32[]{:S(2)}) %collective-permute-start.11) | collective-permute-done | bytes 524320 | tf_op jit(solution)/shard_map/ppermute | solution.py:251
  74.4 2.1 %collective-permute-start.14 = (bf16[128,2048]{1,0:T(8,128)(2,1)S(1)}, bf16[128,2048]{1,0:T(8,128)(2,1)}, u32[]{:S(2)}, u32[]{:S(2)}) collective-permute-start(bf16[128,2048]{1,0:T(8,128)(2,1)S(1)} %add_convert_fusion.2.refs_0_), channel_id=1, source_target_pairs={{0,16},{2,18},{4,20},{6,22},{16,24},{18,26},{20,28},{22,30},{24,8}... | collective-permute-start | bytes 1572872 | tf_op jit(solution)/shard_map/ppermute | solution.py:242
  77.4 4.0 %all-to-all-start.1 = ((f32[32,1,128]{2,1,0:T(1,128)}), f32[32,1,128]{2,1,0:T(1,128)S(1)}, u32[]{:S(2)}, u32[]{:S(2)}) async-start(f32[32,1,128]{2,1,0:T(1,128)} %broadcast_in_dim.90), calls=%async_computation.1 | async-start | bytes 32768 | tf_op jit(solution)/shard_map/all_to_all | solution.py:331
  82.6 1.3 %collective-permute-done.14 = bf16[128,2048]{1,0:T(8,128)(2,1)} collective-permute-done((bf16[128,2048]{1,0:T(8,128)(2,1)S(1)}, bf16[128,2048]{1,0:T(8,128)(2,1)}, u32[]{:S(2)}, u32[]{:S(2)}) %collective-permute-start.14) | collective-permute-done | bytes 524320 | tf_op jit(solution)/shard_map/ppermute | solution.py:242
  83.8 1.3 %add_convert_fusion.1.refs_0_.refs_1_ = bf16[128,2048]{1,0:T(8,128)(2,1)S(1)} fusion(bf16[128,2048]{1,0:T(8,128)(2,1)} %collective-permute-done.14, bf16[128,2048]{1,0:T(8,128)(2,1)S(1)} %collective-permute-done.10, bf16[128,2048]{1,0:T(8,128)(2,1)S(1)} %get-tuple-element.36), kind=kLoop, calls=%fused_computation.2 | loop fusion | flops 1572864 | bytes 2097152 | tf_op jit(solution)/shard_map/convert_element_type | solution.py:317
  86.2 2.9 %collective-permute-start.16 = (bf16[128,2048]{1,0:T(8,128)(2,1)S(1)}, bf16[128,2048]{1,0:T(8,128)(2,1)S(1)}, u32[]{:S(2)}, u32[]{:S(2)}) collective-permute-start(bf16[128,2048]{1,0:T(8,128)(2,1)S(1)} %tie.10), channel_id=1, source_target_pairs={{0,16},{2,18},{4,20},{6,22},{16,24},{18,26},{20,28},{22,30},{24,8}... | collective-permute-start | bytes 1572872 | tf_op jit(solution)/shard_map/ppermute | solution.py:242
  90.5 7.9 %collective-permute-done.16 = bf16[128,2048]{1,0:T(8,128)(2,1)S(1)} collective-permute-done((bf16[128,2048]{1,0:T(8,128)(2,1)S(1)}, bf16[128,2048]{1,0:T(8,128)(2,1)S(1)}, u32[]{:S(2)}, u32[]{:S(2)}) %collective-permute-start.16) | collective-permute-done | bytes 524320 | tf_op jit(solution)/shard_map/ppermute | solution.py:242
  (61 shorter events, 15.1 us)
Async XLA Ops:
  0.6 37.5 %collective-permute-start.1 = (bf16[2048,768]{1,0:T(8,128)(2,1)}, bf16[2048,768]{1,0:T(8,128)(2,1)}, u32[]{:S(2)}, u32[]{:S(2)}) collective-permute-start(bf16[2048,768]{1,0:T(8,128)(2,1)} %bitcast.38), channel_id=1, source_target_pairs={{0,2},{2,0},{4,6},{6,4},{8,10},{10,8},{12,14},{14,12},{16,18},{18,... | collective-permute-start | bytes 9437192 | tf_op jit(solution)/shard_map/ppermute | solution.py:252
  1.1 37.0 %collective-permute-start.2 = (bf16[2048,768]{1,0:T(8,128)(2,1)}, bf16[2048,768]{1,0:T(8,128)(2,1)}, u32[]{:S(2)}, u32[]{:S(2)}) collective-permute-start(bf16[2048,768]{1,0:T(8,128)(2,1)} %bitcast.40), channel_id=1, source_target_pairs={{0,2},{2,0},{4,6},{6,4},{8,10},{10,8},{12,14},{14,12},{16,18},{18,... | collective-permute-start | bytes 9437192 | tf_op jit(solution)/shard_map/ppermute | solution.py:252
  1.2 36.9 %collective-permute-start.3 = (bf16[768,2048]{1,0:T(8,128)(2,1)}, bf16[768,2048]{1,0:T(8,128)(2,1)}, u32[]{:S(2)}, u32[]{:S(2)}) collective-permute-start(bf16[768,2048]{1,0:T(8,128)(2,1)} %bitcast.42), channel_id=1, source_target_pairs={{0,2},{2,0},{4,6},{6,4},{8,10},{10,8},{12,14},{14,12},{16,18},{18,... | collective-permute-start | bytes 9437192 | tf_op jit(solution)/shard_map/ppermute | solution.py:252
  1.7 19.3 %collective-permute-start = (bf16[128,2048]{1,0:T(8,128)(2,1)}, bf16[128,2048]{1,0:T(8,128)(2,1)S(1)}, u32[]{:S(2)}, u32[]{:S(2)}) collective-permute-start(bf16[128,2048]{1,0:T(8,128)(2,1)} %xa.1), channel_id=1, source_target_pairs={{0,4},{2,6},{4,0},{6,2},{8,12},{10,14},{12,8},{14,10},{16,20},{18,... | collective-permute-start | bytes 1572872 | tf_op jit(solution)/shard_map/ppermute | solution.py:251
  4.2 16.8 %collective-permute-start.4 = (bf16[128,2048]{1,0:T(8,128)(2,1)}, bf16[128,2048]{1,0:T(8,128)(2,1)S(1)}, u32[]{:S(2)}, u32[]{:S(2)}) collective-permute-start(bf16[128,2048]{1,0:T(8,128)(2,1)} %xa.1), channel_id=1, source_target_pairs={{0,16},{2,18},{4,20},{6,22},{16,24},{18,26},{20,28},{22,30},{24,8}... | collective-permute-start | bytes 1572872 | tf_op jit(solution)/shard_map/ppermute | solution.py:242
  9.4 11.0 %all-to-all-start = ((bf16[8,2,128]{2,1,0:T(2,128)(2,1)}), bf16[8,2,128]{2,1,0:T(2,128)(2,1)S(1)}, u32[]{:S(2)}, u32[]{:S(2)}) async-start(bf16[8,2,128]{2,1,0:T(2,128)(2,1)} %reshape.293), calls=%async_computation | async-start | bytes 8192 | tf_op jit(solution)/shard_map/all_to_all | solution.py:262
  21.0 12.9 %collective-permute-start.6 = (bf16[128,2048]{1,0:T(8,128)(2,1)S(1)}, bf16[128,2048]{1,0:T(8,128)(2,1)S(1)}, u32[]{:S(2)}, u32[]{:S(2)}) collective-permute-start(bf16[128,2048]{1,0:T(8,128)(2,1)S(1)} %tie.6.xa), channel_id=1, source_target_pairs={{0,16},{2,18},{4,20},{6,22},{16,24},{18,26},{20,28},{22,30},{24,8}... | collective-permute-start | bytes 1572872 | tf_op jit(solution)/shard_map/ppermute | solution.py:242
  22.7 12.8 %collective-permute-start.5 = (bf16[128,2048]{1,0:T(8,128)(2,1)S(1)}, bf16[128,2048]{1,0:T(8,128)(2,1)S(1)}, u32[]{:S(2)}, u32[]{:S(2)}) collective-permute-start(bf16[128,2048]{1,0:T(8,128)(2,1)S(1)} %tie.6.xa), channel_id=1, source_target_pairs={{0,4},{2,6},{4,0},{6,2},{8,12},{10,14},{12,8},{14,10},{16,20},{18,... | collective-permute-start | bytes 1572872 | tf_op jit(solution)/shard_map/ppermute | solution.py:251
  35.5 6.4 %copy-start.1 = (f32[2048]{0:T(1024)S(1)}, f32[2048]{0:T(1024)}, u32[]{:S(2)}) copy-start(f32[2048]{0:T(1024)} %param.14) | copy-start | bytes 24580
  35.5 14.5 %collective-permute-start.8 = (bf16[128,2048]{1,0:T(8,128)(2,1)S(1)}, bf16[128,2048]{1,0:T(8,128)(2,1)S(1)}, u32[]{:S(2)}, u32[]{:S(2)}) collective-permute-start(bf16[128,2048]{1,0:T(8,128)(2,1)S(1)} %tie.7.after.xa), channel_id=1, source_target_pairs={{0,16},{2,18},{4,20},{6,22},{16,24},{18,26},{20,28},{22,30},{24,8}... | collective-permute-start | bytes 1572872 | tf_op jit(solution)/shard_map/ppermute | solution.py:242
  36.7 12.7 %collective-permute-start.7 = (bf16[128,2048]{1,0:T(8,128)(2,1)S(1)}, bf16[128,2048]{1,0:T(8,128)(2,1)S(1)}, u32[]{:S(2)}, u32[]{:S(2)}) collective-permute-start(bf16[128,2048]{1,0:T(8,128)(2,1)S(1)} %tie.7.after.xa), channel_id=1, source_target_pairs={{0,4},{2,6},{4,0},{6,2},{8,12},{10,14},{12,8},{14,10},{16,20},{18,... | collective-permute-start | bytes 1572872 | tf_op jit(solution)/shard_map/ppermute | solution.py:251
  41.9 8.0 %copy-start = (bf16[128,2048]{1,0:T(8,128)(2,1)S(1)}, bf16[128,2048]{1,0:T(8,128)(2,1)}, u32[]{:S(2)}) copy-start(bf16[128,2048]{1,0:T(8,128)(2,1)} %xa.1) | copy-start | bytes 1572868
  47.6 14.9 %collective-permute-start.12 = (bf16[128,2048]{1,0:T(8,128)(2,1)S(1)}, bf16[128,2048]{1,0:T(8,128)(2,1)S(1)}, u32[]{:S(2)}, u32[]{:S(2)}) collective-permute-start(bf16[128,2048]{1,0:T(8,128)(2,1)S(1)} %get-tuple-element.41), channel_id=1, source_target_pairs={{0,4},{2,6},{4,0},{6,2},{8,12},{10,14},{12,8},{14,10},{16,20},{18,... | collective-permute-start | bytes 1572872 | tf_op jit(solution)/shard_map/ppermute | solution.py:251
  49.4 15.6 %collective-permute-start.9 = (bf16[128,2048]{1,0:T(8,128)(2,1)S(1)}, bf16[128,2048]{1,0:T(8,128)(2,1)S(1)}, u32[]{:S(2)}, u32[]{:S(2)}) collective-permute-start(bf16[128,2048]{1,0:T(8,128)(2,1)S(1)} %collective-permute-done.7.refs_0_.xb), channel_id=1, source_target_pairs={{0,16},{2,18},{4,20},{6,22},{16,24},{18,26},{20,28},{22,30},{24,8}... | collective-permute-start | bytes 1572872 | tf_op jit(solution)/shard_map/ppermute | solution.py:242
  61.3 12.4 %collective-permute-start.11 = (bf16[128,2048]{1,0:T(8,128)(2,1)S(1)}, bf16[128,2048]{1,0:T(8,128)(2,1)S(1)}, u32[]{:S(2)}, u32[]{:S(2)}) collective-permute-start(bf16[128,2048]{1,0:T(8,128)(2,1)S(1)} %get-tuple-element.39), channel_id=1, source_target_pairs={{0,4},{2,6},{4,0},{6,2},{8,12},{10,14},{12,8},{14,10},{16,20},{18,... | collective-permute-start | bytes 1572872 | tf_op jit(solution)/shard_map/ppermute | solution.py:251
  62.6 11.5 %collective-permute-start.13 = (bf16[128,2048]{1,0:T(8,128)(2,1)S(1)}, bf16[128,2048]{1,0:T(8,128)(2,1)S(1)}, u32[]{:S(2)}, u32[]{:S(2)}) collective-permute-start(bf16[128,2048]{1,0:T(8,128)(2,1)S(1)} %add_convert_fusion.3), channel_id=1, source_target_pairs={{0,16},{2,18},{4,20},{6,22},{16,24},{18,26},{20,28},{22,30},{24,8}... | collective-permute-start | bytes 1572872 | tf_op jit(solution)/shard_map/ppermute | solution.py:242
  70.7 11.9 %collective-permute-start.10 = (bf16[128,2048]{1,0:T(8,128)(2,1)S(1)}, bf16[128,2048]{1,0:T(8,128)(2,1)S(1)}, u32[]{:S(2)}, u32[]{:S(2)}) collective-permute-start(bf16[128,2048]{1,0:T(8,128)(2,1)S(1)} %get-tuple-element.37), channel_id=1, source_target_pairs={{0,4},{2,6},{4,0},{6,2},{8,12},{10,14},{12,8},{14,10},{16,20},{18,... | collective-permute-start | bytes 1572872 | tf_op jit(solution)/shard_map/ppermute | solution.py:251
  74.4 9.5 %collective-permute-start.14 = (bf16[128,2048]{1,0:T(8,128)(2,1)S(1)}, bf16[128,2048]{1,0:T(8,128)(2,1)}, u32[]{:S(2)}, u32[]{:S(2)}) collective-permute-start(bf16[128,2048]{1,0:T(8,128)(2,1)S(1)} %add_convert_fusion.2.refs_0_), channel_id=1, source_target_pairs={{0,16},{2,18},{4,20},{6,22},{16,24},{18,26},{20,28},{22,30},{24,8}... | collective-permute-start | bytes 1572872 | tf_op jit(solution)/shard_map/ppermute | solution.py:242
  77.4 11.6 %all-to-all-start.1 = ((f32[32,1,128]{2,1,0:T(1,128)}), f32[32,1,128]{2,1,0:T(1,128)S(1)}, u32[]{:S(2)}, u32[]{:S(2)}) async-start(f32[32,1,128]{2,1,0:T(1,128)} %broadcast_in_dim.90), calls=%async_computation.1 | async-start | bytes 32768 | tf_op jit(solution)/shard_map/all_to_all | solution.py:331
  85.1 13.2 %collective-permute-start.15 = (bf16[128,2048]{1,0:T(8,128)(2,1)S(1)}, bf16[128,2048]{1,0:T(8,128)(2,1)S(1)}, u32[]{:S(2)}, u32[]{:S(2)}) collective-permute-start(bf16[128,2048]{1,0:T(8,128)(2,1)S(1)} %tie.9.refs_0_), channel_id=1, source_target_pairs={{0,4},{2,6},{4,0},{6,2},{8,12},{10,14},{12,8},{14,10},{16,20},{18,... | collective-permute-start | bytes 1572872 | tf_op jit(solution)/shard_map/ppermute | solution.py:251
  86.2 12.1 %collective-permute-start.16 = (bf16[128,2048]{1,0:T(8,128)(2,1)S(1)}, bf16[128,2048]{1,0:T(8,128)(2,1)S(1)}, u32[]{:S(2)}, u32[]{:S(2)}) collective-permute-start(bf16[128,2048]{1,0:T(8,128)(2,1)S(1)} %tie.10), channel_id=1, source_target_pairs={{0,16},{2,18},{4,20},{6,22},{16,24},{18,26},{20,28},{22,30},{24,8}... | collective-permute-start | bytes 1572872 | tf_op jit(solution)/shard_map/ppermute | solution.py:242

commit v3 on v2

--- a/solution.py
+++ b/solution.py
@@ -134,10 +134,13 @@
     for copy in x_copies:
         copy.wait()
     for e, (wg, wu) in enumerate(((wg0, wu0), (wg1, wu1))):
-        gate_part = jnp.dot(rows[...], wg[...], preferred_element_type=jnp.float32)
-        up_part = jnp.dot(rows[...], wu[...], preferred_element_type=jnp.float32)
-        value = gate_part / (1.0 + jnp.exp(-gate_part)) * up_part
-        hidden[e] = value.astype(jnp.bfloat16)
+        ff_tile = tile_of(wg.shape[1], 256)
+        for j in range(wg.shape[1] // ff_tile):
+            columns = pl.ds(j * ff_tile, ff_tile)
+            gate_part = jnp.dot(rows[...], wg[:, columns], preferred_element_type=jnp.float32)
+            up_part = jnp.dot(rows[...], wu[:, columns], preferred_element_type=jnp.float32)
+            value = gate_part / (1.0 + jnp.exp(-gate_part)) * up_part
+            hidden[e, :, columns] = value.astype(jnp.bfloat16)
 
     totals = [jnp.zeros((1, LANES), jnp.float32) for _ in range(2 * local)]
     for j in range(width // out_tile):

time: 99.7 us -> 99.8 us (level)
  transfers between devices with their start and end apart: 19 -> 19, of which waited for: 9 -> 9; matrix products, arithmetic and copies ran while one was open for 7% -> 7% of each run, Pallas kernels for 30% -> 31%
where the time goes in v3:
time: 99.8 us; the launch traced here: 99.5 us
  Pallas kernels  30.5 us (31%)
  starting transfers between devices  30.3 us (30%)
  waiting for transfers between devices  28.9 us (29%)
  other arithmetic  5.5 us (6%)
  local copies, waits for them, and re-layouts  2.77 us (3%)
  between operations  1.56 us (2%)
    pallas_call x4, Pallas kernels, expert_call(): pl.pallas_call(functools.partial(expert_kernel, slot), in_specs=[anywhere...  22.9 us
    ppermute x7, waiting for transfers between devices, dense_shards(): lax.ppermute(v, 'ep', [(4 * places[n] + i, 4 * places[(n + 1) % ring] + i...  15.6 us
    ppermute x7, starting transfers between devices, dense_shards(): lax.ppermute(v, 'ep', [(4 * places[n] + i, 4 * places[(n + 1) % ring] + i...  12.6 us
    ppermute x7, starting transfers between devices, dense_shards(): lax.ppermute(v, 'ep', [(i, i ^ 2) for i in range(experts)])  9.24 us
    all_to_all x1, waiting for transfers between devices, dense_shards(): lax.all_to_all(sent_gates, 'ep', split_axis=0, concat_axis=0, tiled=True,...  7.57 us
    pallas_call x2, Pallas kernels, load(): pl.pallas_call(functools.partial(load_kernel, len(arrays)), in_specs=[pl....  7.56 us
    ppermute x7, waiting for transfers between devices, dense_shards(): lax.ppermute(v, 'ep', [(i, i ^ 2) for i in range(experts)])  5.74 us
    all_to_all x1, starting transfers between devices, dense_shards(): lax.all_to_all(jnp.broadcast_to(told, (experts * groups, told.shape[1])),...  4.05 us
  transfers between devices with their start and end apart: 19, of which 9 were waited for; matrix products, arithmetic and copies ran while one was open for 7% of the time, Pallas kernels for 31%

profile of v3, /device:TPU:0, one launch (start us, length us, event | category | flops | bytes accessed | tf_op | source)
XLA Modules:
  0.0 99.5 jit_solution(10764156616413105596)
XLA Ops:
  1.7 2.6 %collective-permute-start = (bf16[128,2048]{1,0:T(8,128)(2,1)}, bf16[128,2048]{1,0:T(8,128)(2,1)S(1)}, u32[]{:S(2)}, u32[]{:S(2)}) collective-permute-start(bf16[128,2048]{1,0:T(8,128)(2,1)} %xa.1), channel_id=1, source_target_pairs={{0,4},{2,6},{4,0},{6,2},{8,12},{10,14},{12,8},{14,10},{16,20},{18,... | collective-permute-start | bytes 1572872 | tf_op jit(solution)/shard_map/ppermute | solution.py:254
  4.2 2.6 %collective-permute-start.4 = (bf16[128,2048]{1,0:T(8,128)(2,1)}, bf16[128,2048]{1,0:T(8,128)(2,1)S(1)}, u32[]{:S(2)}, u32[]{:S(2)}) collective-permute-start(bf16[128,2048]{1,0:T(8,128)(2,1)} %xa.1), channel_id=1, source_target_pairs={{0,16},{2,18},{4,20},{6,22},{16,24},{18,26},{20,28},{22,30},{24,8}... | collective-permute-start | bytes 1572872 | tf_op jit(solution)/shard_map/ppermute | solution.py:245
  9.4 3.3 %all-to-all-start = ((bf16[8,2,128]{2,1,0:T(2,128)(2,1)}), bf16[8,2,128]{2,1,0:T(2,128)(2,1)S(1)}, u32[]{:S(2)}, u32[]{:S(2)}) async-start(bf16[8,2,128]{2,1,0:T(2,128)(2,1)} %reshape.293), calls=%async_computation | async-start | bytes 8192 | tf_op jit(solution)/shard_map/all_to_all | solution.py:265
  12.8 7.6 %all-to-all-done = bf16[8,2,128]{2,1,0:T(2,128)(2,1)S(1)} async-done(((bf16[8,2,128]{2,1,0:T(2,128)(2,1)}), bf16[8,2,128]{2,1,0:T(2,128)(2,1)S(1)}, u32[]{:S(2)}, u32[]{:S(2)}) %all-to-all-start) | async-done | bytes 4128 | tf_op jit(solution)/shard_map/all_to_all | solution.py:265
  21.0 1.7 %collective-permute-start.6 = (bf16[128,2048]{1,0:T(8,128)(2,1)S(1)}, bf16[128,2048]{1,0:T(8,128)(2,1)S(1)}, u32[]{:S(2)}, u32[]{:S(2)}) collective-permute-start(bf16[128,2048]{1,0:T(8,128)(2,1)S(1)} %tie.6.xa), channel_id=1, source_target_pairs={{0,16},{2,18},{4,20},{6,22},{16,24},{18,26},{20,28},{22,30},{24,8}... | collective-permute-start | bytes 1572872 | tf_op jit(solution)/shard_map/ppermute | solution.py:245
  22.7 1.4 %collective-permute-start.5 = (bf16[128,2048]{1,0:T(8,128)(2,1)S(1)}, bf16[128,2048]{1,0:T(8,128)(2,1)S(1)}, u32[]{:S(2)}, u32[]{:S(2)}) collective-permute-start(bf16[128,2048]{1,0:T(8,128)(2,1)S(1)} %tie.6.xa), channel_id=1, source_target_pairs={{0,4},{2,6},{4,0},{6,2},{8,12},{10,14},{12,8},{14,10},{16,20},{18,... | collective-permute-start | bytes 1572872 | tf_op jit(solution)/shard_map/ppermute | solution.py:254
  24.1 3.8 %load.2 = (bf16[2048,768]{1,0:T(8,128)(2,1)S(1)}, bf16[2048,768]{1,0:T(8,128)(2,1)S(1)}, bf16[768,2048]{1,0:T(8,128)(2,1)S(1)}) custom-call(f32[8,256]{1,0:T(8,128)S(1)} %gather_fusion, bf16[2048,768]{1,0:T(8,128)(2,1)} %bitcast.39, bf16[2048,768]{1,0:T(8,128)(2,1)} %bitcast.41, bf16[768,2048]{1,0:T(8,128)(2,1)} %bitcast.43), custom_call_target="tpu_custom_call" | custom-call | tf_op jit(solution)/shard_map/load/pallas_call | solution.py:179
  27.9 6.1 %collective-permute-done.6.refs_2_ = bf16[128,2048]{1,0:T(8,128)(2,1)S(1)} collective-permute-done((bf16[128,2048]{1,0:T(8,128)(2,1)S(1)}, bf16[128,2048]{1,0:T(8,128)(2,1)S(1)}, u32[]{:S(2)}, u32[]{:S(2)}) %collective-permute-start.6) | collective-permute-done | bytes 524320 | tf_op jit(solution)/shard_map/ppermute | solution.py:245
  34.0 1.5 %collective-permute-done.5.refs_0_.xb = bf16[128,2048]{1,0:T(8,128)(2,1)S(1)} collective-permute-done((bf16[128,2048]{1,0:T(8,128)(2,1)S(1)}, bf16[128,2048]{1,0:T(8,128)(2,1)S(1)}, u32[]{:S(2)}, u32[]{:S(2)}) %collective-permute-start.5) | collective-permute-done | bytes 524320 | tf_op jit(solution)/shard_map/ppermute | solution.py:254
  36.7 1.4 %collective-permute-start.7 = (bf16[128,2048]{1,0:T(8,128)(2,1)S(1)}, bf16[128,2048]{1,0:T(8,128)(2,1)S(1)}, u32[]{:S(2)}, u32[]{:S(2)}) collective-permute-start(bf16[128,2048]{1,0:T(8,128)(2,1)S(1)} %tie.7.after.xa), channel_id=1, source_target_pairs={{0,4},{2,6},{4,0},{6,2},{8,12},{10,14},{12,8},{14,10},{16,20},{18,... | collective-permute-start | bytes 1572872 | tf_op jit(solution)/shard_map/ppermute | solution.py:254
  38.1 3.8 %load.3 = (bf16[2048,768]{1,0:T(8,128)(2,1)S(1)}, bf16[2048,768]{1,0:T(8,128)(2,1)S(1)}, bf16[768,2048]{1,0:T(8,128)(2,1)S(1)}) custom-call(f32[8,256]{1,0:T(8,128)S(1)} %gather_fusion, bf16[2048,768]{1,0:T(8,128)(2,1)} %collective-permute-done.1.refs_1_, bf16[2048,768]{1,0:T(8,128)(2,1)} %collective-permute-done.2.refs_2_, ...), custom_call_target="tpu_custom_call" | custom-call | tf_op jit(solution)/shard_map/load/pallas_call | solution.py:179
  42.0 5.7 %expert.4 = (bf16[128,2048]{1,0:T(8,128)(2,1)S(1)}, bf16[128,2048]{1,0:T(8,128)(2,1)S(1)}, f32[2,128]{1,0:T(2,128)S(1)}, f32[8,128]{1,0:T(8,128)S(1)}) custom-call(bf16[128,2048]{1,0:T(8,128)(2,1)S(1)} %tie.6.xa, bf16[128,2048]{1,0:T(8,128)(2,1)S(1)} %collective-permute-done.5.refs_0_.xb, ...), custom_call_target="tpu_custom_call", output_to_operand_aliasing={{3}: (11, {})} | custom-call | flops 1 | bytes 1 | tf_op jit(solution)/shard_map/expert/pallas_call | solution.py:214
  49.9 5.7 %expert.5 = (bf16[128,2048]{1,0:T(8,128)(2,1)S(1)}, bf16[128,2048]{1,0:T(8,128)(2,1)S(1)}, f32[2,128]{1,0:T(2,128)S(1)}, f32[8,128]{1,0:T(8,128)S(1)}) custom-call(bf16[128,2048]{1,0:T(8,128)(2,1)S(1)} %copy-done, bf16[128,2048]{1,0:T(8,128)(2,1)S(1)} %collective-permute-done.refs_0_.xb, ...), custom_call_target="tpu_custom_call", output_to_operand_aliasing={{3}: (11, {})} | custom-call | flops 1 | bytes 1 | tf_op jit(solution)/shard_map/expert/pallas_call | solution.py:214
  55.7 5.7 %expert.6 = (bf16[128,2048]{1,0:T(8,128)(2,1)S(1)}, bf16[128,2048]{1,0:T(8,128)(2,1)S(1)}, f32[2,128]{1,0:T(2,128)S(1)}, f32[8,128]{1,0:T(8,128)S(1)}) custom-call(bf16[128,2048]{1,0:T(8,128)(2,1)S(1)} %tie.7.after.xa, bf16[128,2048]{1,0:T(8,128)(2,1)S(1)} %collective-permute-done.7.refs_0_.xb, ...), custom_call_target="tpu_custom_call", output_to_operand_aliasing={{3}: (11, {})} | custom-call | flops 1 | bytes 1 | tf_op jit(solution)/shard_map/expert/pallas_call | solution.py:214
  62.7 1.7 %collective-permute-start.13 = (bf16[128,2048]{1,0:T(8,128)(2,1)S(1)}, bf16[128,2048]{1,0:T(8,128)(2,1)S(1)}, u32[]{:S(2)}, u32[]{:S(2)}) collective-permute-start(bf16[128,2048]{1,0:T(8,128)(2,1)S(1)} %add_convert_fusion.3), channel_id=1, source_target_pairs={{0,16},{2,18},{4,20},{6,22},{16,24},{18,26},{20,28},{22,30},{24,8}... | collective-permute-start | bytes 1572872 | tf_op jit(solution)/shard_map/ppermute | solution.py:245
  65.1 5.7 %expert.7 = (bf16[128,2048]{1,0:T(8,128)(2,1)S(1)}, bf16[128,2048]{1,0:T(8,128)(2,1)S(1)}, f32[2,128]{1,0:T(2,128)S(1)}, bf16[128,2048]{1,0:T(8,128)(2,1)S(1)}) custom-call(bf16[128,2048]{1,0:T(8,128)(2,1)S(1)} %tie.8.after.xa, bf16[128,2048]{1,0:T(8,128)(2,1)S(1)} %collective-permute-done.9.xb, ...), custom_call_target="tpu_custom_call", output_to_operand_aliasing={{3}: (11, {})} | custom-call | flops 1 | bytes 1 | tf_op jit(solution)/shard_map/expert/pallas_call | solution.py:214
  71.8 2.0 %collective-permute-done.11 = bf16[128,2048]{1,0:T(8,128)(2,1)S(1)} collective-permute-done((bf16[128,2048]{1,0:T(8,128)(2,1)S(1)}, bf16[128,2048]{1,0:T(8,128)(2,1)S(1)}, u32[]{:S(2)}, u32[]{:S(2)}) %collective-permute-start.11) | collective-permute-done | bytes 524320 | tf_op jit(solution)/shard_map/ppermute | solution.py:254
  74.4 2.1 %collective-permute-start.14 = (bf16[128,2048]{1,0:T(8,128)(2,1)S(1)}, bf16[128,2048]{1,0:T(8,128)(2,1)}, u32[]{:S(2)}, u32[]{:S(2)}) collective-permute-start(bf16[128,2048]{1,0:T(8,128)(2,1)S(1)} %add_convert_fusion.2.refs_0_), channel_id=1, source_target_pairs={{0,16},{2,18},{4,20},{6,22},{16,24},{18,26},{20,28},{22,30},{24,8}... | collective-permute-start | bytes 1572872 | tf_op jit(solution)/shard_map/ppermute | solution.py:245
  77.5 4.0 %all-to-all-start.1 = ((f32[32,1,128]{2,1,0:T(1,128)}), f32[32,1,128]{2,1,0:T(1,128)S(1)}, u32[]{:S(2)}, u32[]{:S(2)}) async-start(f32[32,1,128]{2,1,0:T(1,128)} %broadcast_in_dim.90), calls=%async_computation.1 | async-start | bytes 32768 | tf_op jit(solution)/shard_map/all_to_all | solution.py:334
  81.6 1.2 %collective-permute-done.10 = bf16[128,2048]{1,0:T(8,128)(2,1)S(1)} collective-permute-done((bf16[128,2048]{1,0:T(8,128)(2,1)S(1)}, bf16[128,2048]{1,0:T(8,128)(2,1)S(1)}, u32[]{:S(2)}, u32[]{:S(2)}) %collective-permute-start.10) | collective-permute-done | bytes 524320 | tf_op jit(solution)/shard_map/ppermute | solution.py:254
  82.8 1.3 %collective-permute-done.14 = bf16[128,2048]{1,0:T(8,128)(2,1)} collective-permute-done((bf16[128,2048]{1,0:T(8,128)(2,1)S(1)}, bf16[128,2048]{1,0:T(8,128)(2,1)}, u32[]{:S(2)}, u32[]{:S(2)}) %collective-permute-start.14) | collective-permute-done | bytes 524320 | tf_op jit(solution)/shard_map/ppermute | solution.py:245
  84.1 1.3 %add_convert_fusion.1.refs_0_.refs_1_ = bf16[128,2048]{1,0:T(8,128)(2,1)S(1)} fusion(bf16[128,2048]{1,0:T(8,128)(2,1)} %collective-permute-done.14, bf16[128,2048]{1,0:T(8,128)(2,1)S(1)} %collective-permute-done.10, bf16[128,2048]{1,0:T(8,128)(2,1)S(1)} %get-tuple-element.36), kind=kLoop, calls=%fused_computation.2 | loop fusion | flops 1572864 | bytes 2097152 | tf_op jit(solution)/shard_map/convert_element_type | solution.py:320
  86.4 2.7 %collective-permute-start.16 = (bf16[128,2048]{1,0:T(8,128)(2,1)S(1)}, bf16[128,2048]{1,0:T(8,128)(2,1)S(1)}, u32[]{:S(2)}, u32[]{:S(2)}) collective-permute-start(bf16[128,2048]{1,0:T(8,128)(2,1)S(1)} %tie.10), channel_id=1, source_target_pairs={{0,16},{2,18},{4,20},{6,22},{16,24},{18,26},{20,28},{22,30},{24,8}... | collective-permute-start | bytes 1572872 | tf_op jit(solution)/shard_map/ppermute | solution.py:245
  90.5 7.9 %collective-permute-done.16 = bf16[128,2048]{1,0:T(8,128)(2,1)S(1)} collective-permute-done((bf16[128,2048]{1,0:T(8,128)(2,1)S(1)}, bf16[128,2048]{1,0:T(8,128)(2,1)S(1)}, u32[]{:S(2)}, u32[]{:S(2)}) %collective-permute-start.16) | collective-permute-done | bytes 524320 | tf_op jit(solution)/shard_map/ppermute | solution.py:245
  (61 shorter events, 15.0 us)
Async XLA Ops:
  0.6 37.5 %collective-permute-start.1 = (bf16[2048,768]{1,0:T(8,128)(2,1)}, bf16[2048,768]{1,0:T(8,128)(2,1)}, u32[]{:S(2)}, u32[]{:S(2)}) collective-permute-start(bf16[2048,768]{1,0:T(8,128)(2,1)} %bitcast.38), channel_id=1, source_target_pairs={{0,2},{2,0},{4,6},{6,4},{8,10},{10,8},{12,14},{14,12},{16,18},{18,... | collective-permute-start | bytes 9437192 | tf_op jit(solution)/shard_map/ppermute | solution.py:255
  1.1 37.0 %collective-permute-start.2 = (bf16[2048,768]{1,0:T(8,128)(2,1)}, bf16[2048,768]{1,0:T(8,128)(2,1)}, u32[]{:S(2)}, u32[]{:S(2)}) collective-permute-start(bf16[2048,768]{1,0:T(8,128)(2,1)} %bitcast.40), channel_id=1, source_target_pairs={{0,2},{2,0},{4,6},{6,4},{8,10},{10,8},{12,14},{14,12},{16,18},{18,... | collective-permute-start | bytes 9437192 | tf_op jit(solution)/shard_map/ppermute | solution.py:255
  1.2 36.9 %collective-permute-start.3 = (bf16[768,2048]{1,0:T(8,128)(2,1)}, bf16[768,2048]{1,0:T(8,128)(2,1)}, u32[]{:S(2)}, u32[]{:S(2)}) collective-permute-start(bf16[768,2048]{1,0:T(8,128)(2,1)} %bitcast.42), channel_id=1, source_target_pairs={{0,2},{2,0},{4,6},{6,4},{8,10},{10,8},{12,14},{14,12},{16,18},{18,... | collective-permute-start | bytes 9437192 | tf_op jit(solution)/shard_map/ppermute | solution.py:255
  1.7 19.3 %collective-permute-start = (bf16[128,2048]{1,0:T(8,128)(2,1)}, bf16[128,2048]{1,0:T(8,128)(2,1)S(1)}, u32[]{:S(2)}, u32[]{:S(2)}) collective-permute-start(bf16[128,2048]{1,0:T(8,128)(2,1)} %xa.1), channel_id=1, source_target_pairs={{0,4},{2,6},{4,0},{6,2},{8,12},{10,14},{12,8},{14,10},{16,20},{18,... | collective-permute-start | bytes 1572872 | tf_op jit(solution)/shard_map/ppermute | solution.py:254
  4.2 16.8 %collective-permute-start.4 = (bf16[128,2048]{1,0:T(8,128)(2,1)}, bf16[128,2048]{1,0:T(8,128)(2,1)S(1)}, u32[]{:S(2)}, u32[]{:S(2)}) collective-permute-start(bf16[128,2048]{1,0:T(8,128)(2,1)} %xa.1), channel_id=1, source_target_pairs={{0,16},{2,18},{4,20},{6,22},{16,24},{18,26},{20,28},{22,30},{24,8}... | collective-permute-start | bytes 1572872 | tf_op jit(solution)/shard_map/ppermute | solution.py:245
  9.4 11.0 %all-to-all-start = ((bf16[8,2,128]{2,1,0:T(2,128)(2,1)}), bf16[8,2,128]{2,1,0:T(2,128)(2,1)S(1)}, u32[]{:S(2)}, u32[]{:S(2)}) async-start(bf16[8,2,128]{2,1,0:T(2,128)(2,1)} %reshape.293), calls=%async_computation | async-start | bytes 8192 | tf_op jit(solution)/shard_map/all_to_all | solution.py:265
  21.0 12.9 %collective-permute-start.6 = (bf16[128,2048]{1,0:T(8,128)(2,1)S(1)}, bf16[128,2048]{1,0:T(8,128)(2,1)S(1)}, u32[]{:S(2)}, u32[]{:S(2)}) collective-permute-start(bf16[128,2048]{1,0:T(8,128)(2,1)S(1)} %tie.6.xa), channel_id=1, source_target_pairs={{0,16},{2,18},{4,20},{6,22},{16,24},{18,26},{20,28},{22,30},{24,8}... | collective-permute-start | bytes 1572872 | tf_op jit(solution)/shard_map/ppermute | solution.py:245
  22.7 12.8 %collective-permute-start.5 = (bf16[128,2048]{1,0:T(8,128)(2,1)S(1)}, bf16[128,2048]{1,0:T(8,128)(2,1)S(1)}, u32[]{:S(2)}, u32[]{:S(2)}) collective-permute-start(bf16[128,2048]{1,0:T(8,128)(2,1)S(1)} %tie.6.xa), channel_id=1, source_target_pairs={{0,4},{2,6},{4,0},{6,2},{8,12},{10,14},{12,8},{14,10},{16,20},{18,... | collective-permute-start | bytes 1572872 | tf_op jit(solution)/shard_map/ppermute | solution.py:254
  35.5 6.4 %copy-start.1 = (f32[2048]{0:T(1024)S(1)}, f32[2048]{0:T(1024)}, u32[]{:S(2)}) copy-start(f32[2048]{0:T(1024)} %param.14) | copy-start | bytes 24580
  35.5 14.4 %collective-permute-start.8 = (bf16[128,2048]{1,0:T(8,128)(2,1)S(1)}, bf16[128,2048]{1,0:T(8,128)(2,1)S(1)}, u32[]{:S(2)}, u32[]{:S(2)}) collective-permute-start(bf16[128,2048]{1,0:T(8,128)(2,1)S(1)} %tie.7.after.xa), channel_id=1, source_target_pairs={{0,16},{2,18},{4,20},{6,22},{16,24},{18,26},{20,28},{22,30},{24,8}... | collective-permute-start | bytes 1572872 | tf_op jit(solution)/shard_map/ppermute | solution.py:245
  36.7 12.6 %collective-permute-start.7 = (bf16[128,2048]{1,0:T(8,128)(2,1)S(1)}, bf16[128,2048]{1,0:T(8,128)(2,1)S(1)}, u32[]{:S(2)}, u32[]{:S(2)}) collective-permute-start(bf16[128,2048]{1,0:T(8,128)(2,1)S(1)} %tie.7.after.xa), channel_id=1, source_target_pairs={{0,4},{2,6},{4,0},{6,2},{8,12},{10,14},{12,8},{14,10},{16,20},{18,... | collective-permute-start | bytes 1572872 | tf_op jit(solution)/shard_map/ppermute | solution.py:254
  41.9 8.0 %copy-start = (bf16[128,2048]{1,0:T(8,128)(2,1)S(1)}, bf16[128,2048]{1,0:T(8,128)(2,1)}, u32[]{:S(2)}) copy-start(bf16[128,2048]{1,0:T(8,128)(2,1)} %xa.1) | copy-start | bytes 1572868
  47.7 14.9 %collective-permute-start.12 = (bf16[128,2048]{1,0:T(8,128)(2,1)S(1)}, bf16[128,2048]{1,0:T(8,128)(2,1)S(1)}, u32[]{:S(2)}, u32[]{:S(2)}) collective-permute-start(bf16[128,2048]{1,0:T(8,128)(2,1)S(1)} %get-tuple-element.41), channel_id=1, source_target_pairs={{0,4},{2,6},{4,0},{6,2},{8,12},{10,14},{12,8},{14,10},{16,20},{18,... | collective-permute-start | bytes 1572872 | tf_op jit(solution)/shard_map/ppermute | solution.py:254
  49.3 15.8 %collective-permute-start.9 = (bf16[128,2048]{1,0:T(8,128)(2,1)S(1)}, bf16[128,2048]{1,0:T(8,128)(2,1)S(1)}, u32[]{:S(2)}, u32[]{:S(2)}) collective-permute-start(bf16[128,2048]{1,0:T(8,128)(2,1)S(1)} %collective-permute-done.7.refs_0_.xb), channel_id=1, source_target_pairs={{0,16},{2,18},{4,20},{6,22},{16,24},{18,26},{20,28},{22,30},{24,8}... | collective-permute-start | bytes 1572872 | tf_op jit(solution)/shard_map/ppermute | solution.py:245
  61.4 12.5 %collective-permute-start.11 = (bf16[128,2048]{1,0:T(8,128)(2,1)S(1)}, bf16[128,2048]{1,0:T(8,128)(2,1)S(1)}, u32[]{:S(2)}, u32[]{:S(2)}) collective-permute-start(bf16[128,2048]{1,0:T(8,128)(2,1)S(1)} %get-tuple-element.39), channel_id=1, source_target_pairs={{0,4},{2,6},{4,0},{6,2},{8,12},{10,14},{12,8},{14,10},{16,20},{18,... | collective-permute-start | bytes 1572872 | tf_op jit(solution)/shard_map/ppermute | solution.py:254
  62.7 11.5 %collective-permute-start.13 = (bf16[128,2048]{1,0:T(8,128)(2,1)S(1)}, bf16[128,2048]{1,0:T(8,128)(2,1)S(1)}, u32[]{:S(2)}, u32[]{:S(2)}) collective-permute-start(bf16[128,2048]{1,0:T(8,128)(2,1)S(1)} %add_convert_fusion.3), channel_id=1, source_target_pairs={{0,16},{2,18},{4,20},{6,22},{16,24},{18,26},{20,28},{22,30},{24,8}... | collective-permute-start | bytes 1572872 | tf_op jit(solution)/shard_map/ppermute | solution.py:245
  70.9 11.9 %collective-permute-start.10 = (bf16[128,2048]{1,0:T(8,128)(2,1)S(1)}, bf16[128,2048]{1,0:T(8,128)(2,1)S(1)}, u32[]{:S(2)}, u32[]{:S(2)}) collective-permute-start(bf16[128,2048]{1,0:T(8,128)(2,1)S(1)} %get-tuple-element.37), channel_id=1, source_target_pairs={{0,4},{2,6},{4,0},{6,2},{8,12},{10,14},{12,8},{14,10},{16,20},{18,... | collective-permute-start | bytes 1572872 | tf_op jit(solution)/shard_map/ppermute | solution.py:254
  74.4 9.6 %collective-permute-start.14 = (bf16[128,2048]{1,0:T(8,128)(2,1)S(1)}, bf16[128,2048]{1,0:T(8,128)(2,1)}, u32[]{:S(2)}, u32[]{:S(2)}) collective-permute-start(bf16[128,2048]{1,0:T(8,128)(2,1)S(1)} %add_convert_fusion.2.refs_0_), channel_id=1, source_target_pairs={{0,16},{2,18},{4,20},{6,22},{16,24},{18,26},{20,28},{22,30},{24,8}... | collective-permute-start | bytes 1572872 | tf_op jit(solution)/shard_map/ppermute | solution.py:245
  77.5 11.6 %all-to-all-start.1 = ((f32[32,1,128]{2,1,0:T(1,128)}), f32[32,1,128]{2,1,0:T(1,128)S(1)}, u32[]{:S(2)}, u32[]{:S(2)}) async-start(f32[32,1,128]{2,1,0:T(1,128)} %broadcast_in_dim.90), calls=%async_computation.1 | async-start | bytes 32768 | tf_op jit(solution)/shard_map/all_to_all | solution.py:334
  85.4 13.1 %collective-permute-start.15 = (bf16[128,2048]{1,0:T(8,128)(2,1)S(1)}, bf16[128,2048]{1,0:T(8,128)(2,1)S(1)}, u32[]{:S(2)}, u32[]{:S(2)}) collective-permute-start(bf16[128,2048]{1,0:T(8,128)(2,1)S(1)} %tie.9.refs_0_), channel_id=1, source_target_pairs={{0,4},{2,6},{4,0},{6,2},{8,12},{10,14},{12,8},{14,10},{16,20},{18,... | collective-permute-start | bytes 1572872 | tf_op jit(solution)/shard_map/ppermute | solution.py:254
  86.4 12.0 %collective-permute-start.16 = (bf16[128,2048]{1,0:T(8,128)(2,1)S(1)}, bf16[128,2048]{1,0:T(8,128)(2,1)S(1)}, u32[]{:S(2)}, u32[]{:S(2)}) collective-permute-start(bf16[128,2048]{1,0:T(8,128)(2,1)S(1)} %tie.10), channel_id=1, source_target_pairs={{0,16},{2,18},{4,20},{6,22},{16,24},{18,26},{20,28},{22,30},{24,8}... | collective-permute-start | bytes 1572872 | tf_op jit(solution)/shard_map/ppermute | solution.py:245
